TPU v7x, 32 devices: a whole 2x2x4 slice. The times are simulated.
32 devices in a mesh: ba: 2 (over core), row: 4 (over y, x), col: 4 (over z).
Axes of the slice: x: 2, y: 2, z: 4, core: 2. Of those that a mesh axis runs over, the one named last changes fastest.
Arguments:
- tokens: bfloat16 [12288, 768], P(('ba', 'row', 'col')), may hold values from -6 to 6
- lengths: int32 [8, 4], P(('ba', 'row')), may hold values from 1 to 768, 1536 in all within a row
- w_query: bfloat16 [768, 768], P('row', 'col'), may hold values from -0.21875 to 0.21875
- w_key: bfloat16 [768, 768], P('row', 'col'), may hold values from -0.21875 to 0.21875
- w_value: bfloat16 [768, 768], P('row', 'col'), may hold values from -0.21875 to 0.21875
- w_out: bfloat16 [768, 768], P('col', 'row'), may hold values from -1.75 to 1.75
- w_gate: bfloat16 [768, 2048], P('row', 'col'), may hold values from -0.21875 to 0.21875
- w_up: bfloat16 [768, 2048], P('row', 'col'), may hold values from -0.21875 to 0.21875
- w_down: bfloat16 [2048, 768], P('col', 'row'), may hold values from -0.25 to 0.25
- gain_attn: float32 [768], replicated, may hold values from 0.5 to 1.5
- gain_mlp: float32 [768], replicated, may hold values from 0.5 to 1.5
- cotangent: bfloat16 [12288, 768], P(('ba', 'row', 'col')), may hold values from -6 to 6
Outputs:
- layer_out: bfloat16 [12288, 768], P(('ba', 'row', 'col'))
- input_grad: bfloat16 [12288, 768], P(('ba', 'row', 'col'))
- grad_query: float32 [768, 768], P('row', 'col')
- grad_key: float32 [768, 768], P('row', 'col')
- grad_value: float32 [768, 768], P('row', 'col')
- grad_out: float32 [768, 768], P('col', 'row')
- grad_gate: float32 [768, 2048], P('row', 'col')
- grad_up: float32 [768, 2048], P('row', 'col')
- grad_down: float32 [2048, 768], P('col', 'row')
- grad_gain_attn: float32 [768], replicated
- grad_gain_mlp: float32 [768], replicated
Inputs may be any that keep to these rules, and one draw needn't show every extreme that they name: `lengths`: each row sums to 1536, and its largest length is exactly 768.
All inputs are finite; a program needn't handle non-finite values.
Results may differ from a plain program's by a relative error of at most 0.015.
Values may be sent and summed in bfloat16 or wider, within the bound.
No kernel may reach another device: no remote copies, remote signals or barrier semaphores. Data moves between devices by JAX's collectives and lax.ppermute only.
A program may use at most 128 MiB of HBM per device.

v0:
```python
import functools
import jax
import jax.numpy as jnp
from jax import lax
from jax.experimental import pallas as pl
from jax.experimental.pallas import tpu as pltpu
from jax.sharding import PartitionSpec as P

HEAD_DIM = 64
PAIR = 2 * HEAD_DIM
LONGEST = 768
EPSILON = 1e-06
ROPE_BASE = 10000.0
Q_ROWS = 128
NEG = -1e30
SCALE = HEAD_DIM ** (-0.5)
VMEM_LIMIT = 56 * 1024 * 1024
LOW = jnp.bfloat16
COST = pl.CostEstimate(flops=1000, bytes_accessed=1000, transcendentals=0)
F32 = jnp.float32


def contract(left, right, first, second):
    return lax.dot_general(
        left, right, (((first,), (second,)), ((), ())), preferred_element_type=F32
    )


def seq_starts(lengths, places):
    starts = jnp.zeros_like(places)
    end = jnp.int32(0)
    for length in lengths:
        end = end + length
        starts = jnp.where(places >= end, end, starts)
    return starts


def split_heads(pair):
    lane = lax.broadcasted_iota(jnp.int32, pair.shape, 1)
    zero = jnp.zeros_like(pair)
    return jnp.concatenate(
        [jnp.where(lane < HEAD_DIM, pair, zero), jnp.where(lane >= HEAD_DIM, pair, zero)], axis=0
    )


def join_heads(stacked):
    rows = stacked.shape[0] // 2
    lane = lax.broadcasted_iota(jnp.int32, (rows, PAIR), 1)
    return jnp.where(lane < HEAD_DIM, stacked[:rows], stacked[rows:])


def rotate_pair(pair, cosine, sine):
    half = HEAD_DIM // 2
    lane = lax.broadcasted_iota(jnp.int32, pair.shape, 1)
    other = jnp.where(
        lane % HEAD_DIM < half, pltpu.roll(pair, PAIR - half, 1), pltpu.roll(pair, half, 1)
    )
    return pair * cosine + other * sine


class Layout:
    def __init__(self, n_row, n_col, seqs):
        self.n_row, self.n_col, self.seqs = n_row, n_col, seqs

    def lengths(self, info):
        return [info[j] for j in range(self.seqs)]

    def first(self, info):
        return info[self.seqs]

    def core(self, info):
        return info[self.seqs + 1]

    def flip(self, info):
        return info[self.seqs + 2]

    def col(self, info):
        return info[self.seqs + 3]

    def places(self, info, pieces):
        count = self.n_row * self.n_col
        slot = 0
        found = []
        for piece in pieces:
            for index in range(piece.shape[0]):
                core = self.core(info) if slot < count else 1 - self.core(info)
                place = slot % count
                row = jnp.bitwise_xor(jnp.int32(place // self.n_col), self.flip(info))
                step = place % self.n_col
                col = lax.rem(self.col(info) + (self.n_col - step), self.n_col)
                found.append((piece, index, core, row, step, col))
                slot += 1
        return found


def norm_rows(values, gain):
    scale = lax.rsqrt(jnp.mean(values * values, axis=1, keepdims=True) + EPSILON)
    return scale, values * scale * gain


def norm_kernel(x_ref, gain_ref, h_ref):
    _, normed = norm_rows(x_ref[...].astype(F32), gain_ref[...])
    h_ref[...] = normed.astype(LOW)


def norm(tokens, gain):
    vmem = pl.BlockSpec(memory_space=pltpu.VMEM)
    return pl.pallas_call(
        norm_kernel,
        out_shape=jax.ShapeDtypeStruct(tokens.shape, LOW),
        in_specs=[vmem, vmem],
        out_specs=vmem,
        cost_estimate=COST,
        name="norm",
    )(tokens, gain)


def leaver(sems):
    leaving = []

    def leave(source, target):
        copy = pltpu.make_async_copy(source, target, sems.at[len(leaving)])
        copy.start()
        leaving.append(copy)

    return leaving, leave


def project_turned(out, place, h, weight, cosine, sine):
    for first in range(0, weight.shape[1], 2 * PAIR):
        both = contract(h, weight[:, first : first + 2 * PAIR], 1, 0)
        for at in range(0, 2 * PAIR, PAIR):
            out[place, first + at : first + at + PAIR] = rotate_pair(
                both[:, at : at + PAIR], cosine, sine
            ).astype(LOW)


def project_plain(out, place, h, weight):
    for first in range(0, weight.shape[1], 2 * PAIR):
        lanes = slice(first, first + 2 * PAIR)
        out[place, lanes] = contract(h, weight[:, lanes], 1, 0).astype(LOW)


def prepare_kernel(layout, blocks, *refs):
    info = refs[0]
    seen = refs[1 : 1 + blocks]
    cos_ref, sin_ref = refs[1 + blocks : 3 + blocks]
    n_out, n_scratch = 7, 7
    pieces = refs[3 + blocks : -(n_out + n_scratch)]
    outs = refs[-(n_out + n_scratch) : -n_scratch]
    buf, wq, wk, wv, wo, sems, out_sems = refs[-n_scratch:]
    wq_out, wk_out, wv_out, wo_out, q, k, v = outs
    copies = []
    for i, (piece, index, core, row, _, col) in enumerate(layout.places(info, pieces)):
        copy = pltpu.make_async_copy(piece.at[index], buf.at[core, row, col], sems.at[i])
        copy.start()
        copies.append(copy)
    for copy in copies:
        copy.wait()
    leaving, leave = leaver(out_sems)
    deep, wide = buf.shape[3], buf.shape[4] // 2
    for core, pair in enumerate(((wq, wk), (wv, wo))):
        for row in range(layout.n_row):
            for col in range(layout.n_col):
                for part in range(2):
                    pair[part][row * deep : (row + 1) * deep, col * wide : (col + 1) * wide] = buf[
                        core, row, col, :, part * wide : (part + 1) * wide
                    ]
    for source, target in ((wq, wq_out), (wk, wk_out), (wv, wv_out), (wo, wo_out)):
        leave(source, target)
    rows = seen[0].shape[0]
    for j in range(blocks):
        place = slice(j * rows, (j + 1) * rows)
        h = seen[j][...]
        project_turned(k, place, h, wk, cos_ref[place], sin_ref[place])
        project_plain(v, place, h, wv)
        if j == blocks - 1:
            project_turned(q, slice(0, rows), h, wq, cos_ref[place], sin_ref[place])
    for copy in leaving:
        copy.wait()


def prepare(layout, info, seen, cosine, sine, pieces, *deps):
    rows, width = seen[0].shape
    deep, lanes = pieces[0].shape[1:]
    n_blocks = 2 * layout.n_row * layout.n_col
    vmem, anyspace = pl.BlockSpec(memory_space=pltpu.VMEM), pl.BlockSpec(memory_space=pl.ANY)
    shapes = [((width, width), LOW)] * 4 + [((rows, width), LOW)]
    shapes += [((rows * len(seen), width), LOW)] * 2
    count = 3 + len(seen) + len(pieces)
    return pl.pallas_call(
        with_deps(functools.partial(prepare_kernel, layout, len(seen)), count, len(deps)),
        out_shape=tuple(jax.ShapeDtypeStruct(*shape) for shape in shapes),
        in_specs=[pl.BlockSpec(memory_space=pltpu.SMEM)]
        + [vmem] * (len(seen) + 2)
        + [anyspace] * (len(pieces) + len(deps)),
        out_specs=(anyspace,) * 4 + (vmem,) * 3,
        scratch_shapes=[pltpu.VMEM((2, layout.n_row, layout.n_col, deep, lanes), LOW)]
        + [pltpu.VMEM((width, width), LOW)] * 4
        + [pltpu.SemaphoreType.DMA((n_blocks,)), pltpu.SemaphoreType.DMA((4,))],
        compiler_params=pltpu.CompilerParams(vmem_limit_bytes=VMEM_LIMIT),
        cost_estimate=COST,
        name="prepare",
    )(info, *seen, cosine, sine, *pieces, *deps)


def front_kernel(layout, *refs):
    (
        info, far_ref, cos_ref, sin_ref, x_ref, gain_ref, q, k_near, v_near, wk, wv, wo,
        k_out, v_out, heads_out, mid_ref, h2_ref, lse_ref, k, v, heads, near_sems, out_sems,
    ) = refs
    rows, width = x_ref.shape
    arriving = []
    for i, (near, whole) in enumerate(((k_near, k), (v_near, v))):
        copy = pltpu.make_async_copy(
            near, whole.at[pl.ds(rows, near.shape[0])], near_sems.at[i]
        )
        copy.start()
        arriving.append(copy)
    leaving, leave = leaver(out_sems)
    h = far_ref[...]
    place = slice(0, rows)
    project_turned(k, place, h, wk, cos_ref[...], sin_ref[...])
    project_plain(v, place, h, wv)
    for copy in arriving:
        copy.wait()
    leave(k, k_out)
    leave(v, v_out)
    halo = k.shape[0] - rows
    window = halo + Q_ROWS

    @pl.loop(0, rows // Q_ROWS)
    def _(step):
        first_query = layout.first(info) + step * Q_ROWS
        query_place = first_query + lax.broadcasted_iota(jnp.int32, (Q_ROWS, 1), 0)
        start = seq_starts(layout.lengths(info), query_place)
        key_place = first_query - halo + lax.broadcasted_iota(jnp.int32, (Q_ROWS, window), 1)
        bias = jnp.where((key_place >= start) & (key_place <= query_place), 0.0, NEG)
        bias = jnp.concatenate([bias, bias], axis=0)
        first = pl.multiple_of(step * Q_ROWS, Q_ROWS)
        lane = lax.broadcasted_iota(jnp.int32, (Q_ROWS, Q_ROWS), 1)
        table = jnp.zeros((Q_ROWS, Q_ROWS), F32)
        for pair in range(width // PAIR):
            lanes = slice(pair * PAIR, (pair + 1) * PAIR)
            query = split_heads(q[pl.ds(first, Q_ROWS), lanes] * SCALE)
            scores = contract(query, k[pl.ds(first, window), lanes], 1, 1) + bias
            peak = jnp.max(scores, axis=1, keepdims=True)
            weights = jnp.exp(scores - peak)
            total = jnp.sum(weights, axis=1, keepdims=True)
            out = contract(weights.astype(LOW), v[pl.ds(first, window), lanes], 1, 0)
            heads[pl.ds(first, Q_ROWS), lanes] = join_heads(out / total).astype(LOW)
            log_sum = peak + jnp.log(total)
            table = jnp.where(lane == 2 * pair, log_sum[:Q_ROWS], table)
            table = jnp.where(lane == 2 * pair + 1, log_sum[Q_ROWS:], table)
        lse_ref[step] = table.T[: lse_ref.shape[1]]

    leave(heads, heads_out)
    middle = x_ref[...].astype(F32) + contract(heads[...], wo[...], 1, 1)
    mid_ref[...] = middle
    _, normed = norm_rows(middle, gain_ref[...])
    h2_ref[...] = normed.astype(LOW)
    for copy in leaving:
        copy.wait()


def stat_rows(width):
    return -(-(width // HEAD_DIM) // 8) * 8


def front(layout, info, far, cosine, sine, tokens, gain, q, k_near, v_near, wk, wv, wo, *deps):
    rows, width = tokens.shape
    vmem, anyspace = pl.BlockSpec(memory_space=pltpu.VMEM), pl.BlockSpec(memory_space=pl.ANY)
    long = jax.ShapeDtypeStruct((rows + k_near.shape[0], width), LOW)
    low = jax.ShapeDtypeStruct((rows, width), LOW)
    stats = (rows // Q_ROWS, stat_rows(width), Q_ROWS)
    return pl.pallas_call(
        with_deps(functools.partial(front_kernel, layout), 12, len(deps)),
        out_shape=(
            long, long, low, jax.ShapeDtypeStruct((rows, width), F32), low,
            jax.ShapeDtypeStruct(stats, F32),
        ),
        in_specs=[pl.BlockSpec(memory_space=pltpu.SMEM)]
        + [vmem] * 6 + [anyspace] * 2 + [vmem] * 3
        + [anyspace] * len(deps),
        out_specs=(anyspace,) * 3 + (vmem,) * 3,
        scratch_shapes=[
            pltpu.VMEM(long.shape, LOW), pltpu.VMEM(long.shape, LOW), pltpu.VMEM(low.shape, LOW),
            pltpu.SemaphoreType.DMA((2,)), pltpu.SemaphoreType.DMA((3,)),
        ],
        compiler_params=pltpu.CompilerParams(vmem_limit_bytes=VMEM_LIMIT),
        cost_estimate=COST,
        name="front",
    )(info, far, cosine, sine, tokens, gain, q, k_near, v_near, wk, wv, wo, *deps)


def mlp_kernel(layout, *refs):
    info, h_ref, h2_ref, dy_ref, dy2_ref = refs[:5]
    n_out, n_scratch = 6, 4
    pieces = refs[5 : -(n_out + n_scratch)]
    own_out, own_back, send_ref, hid_ref, dgate_ref, dup_ref = refs[
        -(n_out + n_scratch) : -n_scratch
    ]
    weight, acc, acc_back, sems = refs[-n_scratch:]
    rows = h_ref.shape[0]
    deep = pieces[0].shape[1]
    half = weight.shape[2] // 3
    waits = [[] for _ in range(layout.n_col)]
    for i, (piece, index, _, row, step, _) in enumerate(layout.places(info, pieces)):
        copy = pltpu.make_async_copy(
            piece.at[index],
            weight.at[step, pl.ds(pl.multiple_of(row * deep, 16), deep)],
            sems.at[i],
        )
        copy.start()
        waits[step].append(copy)
    tokens = ((h_ref, dy_ref), (h2_ref, dy2_ref))
    for step in range(layout.n_col):
        for copy in waits[step]:
            copy.wait()
        w_in, w_down = slice(0, 2 * half), slice(2 * half, 3 * half)
        lanes = slice(step * half, (step + 1) * half)
        for j, (h, dy) in enumerate(tokens):
            place = slice(j * rows, (j + 1) * rows)
            both = contract(h[...], weight[step, :, w_in], 1, 0)
            grad = contract(dy[...], weight[step, :, w_down], 1, 0)
            gate, up = both[:, :half], both[:, half:]
            sig = jax.nn.sigmoid(gate)
            silu = gate * sig
            hidden = (silu * up).astype(LOW)
            d_gate = (grad * up * (sig + silu * (1.0 - sig))).astype(LOW)
            d_up = (grad * silu).astype(LOW)
            hid_ref[place, lanes] = hidden
            dgate_ref[place, lanes] = d_gate
            dup_ref[place, lanes] = d_up
            out = contract(hidden, weight[step, :, w_down], 1, 1)
            back = contract(
                jnp.concatenate([d_gate, d_up], axis=1), weight[step, :, w_in], 1, 1
            )
            if step == 0:
                acc[place], acc_back[place] = out, back
            elif step < layout.n_col - 1:
                acc[place] += out
                acc_back[place] += back
            elif j == 0:
                own_out[...], own_back[...] = acc[place] + out, acc_back[place] + back
            else:
                send_ref[0] = (acc[place] + out).astype(LOW)
                send_ref[1] = (acc_back[place] + back).astype(LOW)


def mlp(layout, info, h, h_other, dy, dy_other, pieces, *deps):
    rows, width = h.shape
    deep, lanes = pieces[0].shape[1:]
    units = lanes // 3 * layout.n_col
    vmem, anyspace = pl.BlockSpec(memory_space=pltpu.VMEM), pl.BlockSpec(memory_space=pl.ANY)

    def like(shape, dtype):
        return jax.ShapeDtypeStruct(shape, dtype)

    return pl.pallas_call(
        with_deps(functools.partial(mlp_kernel, layout), 5 + len(pieces), len(deps)),
        out_shape=(like((rows, width), F32),) * 2
        + (like((2, rows, width), LOW),)
        + (like((2 * rows, units), LOW),) * 3,
        in_specs=[pl.BlockSpec(memory_space=pltpu.SMEM)]
        + [vmem] * 4
        + [anyspace] * (len(pieces) + len(deps)),
        out_specs=(vmem,) * 6,
        scratch_shapes=[
            pltpu.VMEM((layout.n_col, width, lanes), LOW),
            pltpu.VMEM((2 * rows, width), F32),
            pltpu.VMEM((2 * rows, width), F32),
            pltpu.SemaphoreType.DMA((layout.n_row * layout.n_col,)),
        ],
        compiler_params=pltpu.CompilerParams(vmem_limit_bytes=VMEM_LIMIT),
        cost_estimate=COST,
        name="mlp",
    )(info, h, h_other, dy, dy_other, *pieces, *deps)


def middle_kernel(
    mid_ref, dy_ref, gain_ref, wo_ref, heads_ref, own_out, own_back, got_ref,
    out_ref, dmid_ref, dm_ref, dheads_ref, dgain_ref, inner_ref,
):
    middle = mid_ref[...]
    out_ref[...] = (middle + own_out[...] + got_ref[0].astype(F32)).astype(LOW)
    d_h = own_back[...] + got_ref[1].astype(F32)
    scale = lax.rsqrt(jnp.mean(middle * middle, axis=1, keepdims=True) + EPSILON)
    weighted = d_h * gain_ref[...]
    inner = jnp.mean(weighted * middle, axis=1, keepdims=True)
    d_middle = dy_ref[...].astype(F32) + scale * weighted - middle * (scale**3 * inner)
    dgain_ref[...] = jnp.sum(d_h * middle * scale, axis=0, keepdims=True)
    dmid_ref[...] = d_middle
    d_low = d_middle.astype(LOW)
    dm_ref[...] = d_low
    d_heads = contract(d_low, wo_ref[...], 1, 0).astype(LOW)
    dheads_ref[...] = d_heads
    product = d_heads.astype(F32) * heads_ref[...].astype(F32)
    shape = (inner_ref.shape[1], product.shape[1])
    head = lax.broadcasted_iota(jnp.int32, shape, 1) // HEAD_DIM
    own = (head == lax.broadcasted_iota(jnp.int32, shape, 0)).astype(F32)
    for step in range(inner_ref.shape[0]):
        inner_ref[step] = lax.dot_general(
            own, product[step * Q_ROWS : (step + 1) * Q_ROWS], (((1,), (1,)), ((), ())),
            preferred_element_type=F32, precision=lax.Precision.HIGHEST,
        )


def middle_grads(middle, dy, gain, w_out_t, heads, own_out, own_back, got, *deps):
    rows, width = middle.shape
    vmem = pl.BlockSpec(memory_space=pltpu.VMEM)
    low = jax.ShapeDtypeStruct((rows, width), LOW)
    return pl.pallas_call(
        with_deps(middle_kernel, 8, len(deps)),
        out_shape=(
            low, jax.ShapeDtypeStruct((rows, width), F32), low, low,
            jax.ShapeDtypeStruct((1, width), F32),
            jax.ShapeDtypeStruct((rows // Q_ROWS, stat_rows(width), Q_ROWS), F32),
        ),
        in_specs=[vmem] * 8 + [pl.BlockSpec(memory_space=pl.ANY)] * len(deps),
        out_specs=(vmem,) * 6,
        compiler_params=pltpu.CompilerParams(vmem_limit_bytes=VMEM_LIMIT),
        cost_estimate=COST,
        name="middle_grads",
    )(middle, dy, gain, w_out_t, heads, own_out, own_back, got, *deps)


def grad_slots(layout):
    n_row, n_col = layout.n_row, layout.n_col
    if n_row != 4:
        return {(a, k): (0, (a, k)) for a in range(n_row) for k in range(n_col)}
    cut = n_col // 2
    slots = {}
    for k in range(n_col):
        slots[0, k] = (0, (k,))
        if k < cut:
            slots[1, k], slots[3, k], slots[2, k] = (1, (0, k)), (1, (1, k)), (3, (k,))
        else:
            slots[2, k], slots[3, k] = (2, (0, k - cut)), (2, (1, k - cut))
            slots[1, k] = (4, (k - cut,))
    return slots


def grad_shapes(layout, deep, lanes):
    n_row, n_col = layout.n_row, layout.n_col
    if n_row != 4:
        lead = [(n_row, n_col)]
    else:
        cut = n_col // 2
        lead = [(n_col,), (2, cut), (2, n_col - cut), (cut,), (n_col - cut,)]
    return tuple(jax.ShapeDtypeStruct(first + (deep, lanes), LOW) for first in lead)


def row_of(layout, info, a, deep):
    row = jnp.bitwise_xor(jnp.int32(a), layout.flip(info))
    return pl.ds(pl.multiple_of(row * deep, 16), deep)


def mlp_grads_kernel(layout, info, hid_ref, dgate_ref, dup_ref, h_ref, h2_ref, dy_t, *refs):
    outs, h_t = refs[:-1], refs[-1]
    half = hid_ref.shape[1] // layout.n_col
    deep = outs[0].shape[-2]
    rows = h_ref.shape[0]
    h_t[:, :rows] = h_ref[...].T
    h_t[:, rows:] = h2_ref[...].T
    slots = grad_slots(layout)
    for col in range(layout.n_col):
        step = lax.rem(layout.col(info) + (layout.n_col - col), layout.n_col)
        lanes = pl.ds(pl.multiple_of(step * half, half), half)
        for j, (left, right) in enumerate(((dy_t, hid_ref), (h_t, dgate_ref), (h_t, dup_ref))):
            for a in range(layout.n_row):
                out, index = slots[a, col]
                outs[out][(*index, slice(None), slice(j * half, (j + 1) * half))] = contract(
                    left[row_of(layout, info, a, deep)], right[:, lanes], 1, 0
                ).astype(LOW)


def mlp_grads(layout, info, hidden, d_gate, d_up, h, h_other, dy_t, *deps):
    rows, width = h.shape
    half = hidden.shape[1] // layout.n_col
    vmem = pl.BlockSpec(memory_space=pltpu.VMEM)
    shapes = grad_shapes(layout, width // layout.n_row, 3 * half)
    return pl.pallas_call(
        with_deps(functools.partial(mlp_grads_kernel, layout), 7, len(deps)),
        out_shape=shapes,
        in_specs=[pl.BlockSpec(memory_space=pltpu.SMEM)]
        + [vmem] * 6
        + [pl.BlockSpec(memory_space=pl.ANY)] * len(deps),
        out_specs=(vmem,) * len(shapes),
        scratch_shapes=[pltpu.VMEM((width, 2 * rows), LOW)],
        compiler_params=pltpu.CompilerParams(vmem_limit_bytes=VMEM_LIMIT),
        cost_estimate=COST,
        name="mlp_grads",
    )(info, hidden, d_gate, d_up, h, h_other, dy_t, *deps)


def with_deps(kernel, count, deps):
    def run(*refs):
        kernel(*refs[:count], *refs[count + deps :])

    return run


def turn_kernel(groups, *refs):
    outs = refs[-len(groups) :]
    at = 0
    for count, out in zip(groups, outs):
        first = 0
        for ref in refs[at : at + count]:
            out[:, first : first + ref.shape[0]] = ref[...].T
            first += ref.shape[0]
        at += count


def turn(groups, *deps):
    vmem = pl.BlockSpec(memory_space=pltpu.VMEM)
    arrays = [array for group in groups for array in group]
    counts = [len(group) for group in groups]
    return pl.pallas_call(
        with_deps(functools.partial(turn_kernel, counts), len(arrays), len(deps)),
        out_shape=tuple(
            jax.ShapeDtypeStruct((group[0].shape[1], sum(a.shape[0] for a in group)), LOW)
            for group in groups
        ),
        in_specs=[vmem] * len(arrays) + [pl.BlockSpec(memory_space=pl.ANY)] * len(deps),
        out_specs=(vmem,) * len(groups),
        compiler_params=pltpu.CompilerParams(vmem_limit_bytes=VMEM_LIMIT),
        cost_estimate=COST,
        name="turn",
    )(*arrays, *deps)


def turn_rest_kernel(layout, info, far_ref, far2_ref, dm_ref, dm2_ref, near_t, far_t, short_t):
    rows = far_ref.shape[0]
    for j, ref in enumerate((far_ref, far2_ref)):
        far_t[:, j * rows : (j + 1) * rows] = ref[...].T
    each = near_t.shape[1] // 2

    @pl.when(layout.core(info) == 0)
    def _():
        for j in range(2):
            short_t[:, j * rows : (j + 1) * rows] = near_t[:, (j + 1) * each - rows : (j + 1) * each]

    @pl.when(layout.core(info) == 1)
    def _():
        for j, ref in enumerate((dm_ref, dm2_ref)):
            short_t[:, j * rows : (j + 1) * rows] = ref[...].T


def turn_rest(layout, info, far, far_other, dm, dm_other, near_t, *deps):
    vmem = pl.BlockSpec(memory_space=pltpu.VMEM)
    rows, width = far.shape
    return pl.pallas_call(
        with_deps(functools.partial(turn_rest_kernel, layout), 6, len(deps)),
        out_shape=(jax.ShapeDtypeStruct((width, 2 * rows), LOW),) * 2,
        in_specs=[pl.BlockSpec(memory_space=pltpu.SMEM)]
        + [vmem] * 5
        + [pl.BlockSpec(memory_space=pl.ANY)] * len(deps),
        out_specs=(vmem,) * 2,
        compiler_params=pltpu.CompilerParams(vmem_limit_bytes=VMEM_LIMIT),
        cost_estimate=COST,
        name="turn_rest",
    )(info, far, far_other, dm, dm_other, near_t, *deps)


def attend_backward_kernel(
    layout, info, q_ref, k_ref, v_ref, g_ref, lse_ref, inner_ref, cos_ref, sin_ref, cosq_ref,
    sinq_ref, dq_ref, keep_ref, send_ref, dk_acc, dv_acc,
):
    step = pl.program_id(0)
    steps = pl.num_programs(0)
    halo = k_ref.shape[0] - steps * Q_ROWS
    window = halo + Q_ROWS
    first_query = layout.first(info) + step * Q_ROWS
    query_place = first_query + lax.broadcasted_iota(jnp.int32, (1, Q_ROWS), 1)
    start = seq_starts(layout.lengths(info), query_place)
    key_place = first_query - halo + lax.broadcasted_iota(jnp.int32, (window, Q_ROWS), 0)
    bias = jnp.where((key_place >= start) & (key_place <= query_place), 0.0, NEG)
    bias = jnp.concatenate([bias, bias], axis=1)
    first = pl.multiple_of(step * Q_ROWS, Q_ROWS)

    @pl.when(step == 0)
    def _():
        dk_acc[...] = jnp.zeros_like(dk_acc)
        dv_acc[...] = jnp.zeros_like(dv_acc)

    def both(ref, pair):
        head = info[layout.seqs + 4] + 2 * pair
        return jnp.concatenate([ref[0, pl.ds(head, 1)], ref[0, pl.ds(head + 1, 1)]], axis=1)

    cosine, sine = cosq_ref[...], -sinq_ref[...]
    pairs = q_ref.shape[1] // PAIR
    for pair in range(pairs):
        lanes = slice(pair * PAIR, (pair + 1) * PAIR)
        query = split_heads(q_ref[:, lanes] * SCALE)
        grad = split_heads(g_ref[:, lanes])
        keys = k_ref[pl.ds(first, window), lanes]
        probs = jnp.exp(contract(keys, query, 1, 1) + bias - both(lse_ref, pair))
        grad_probs = contract(v_ref[pl.ds(first, window), lanes], grad, 1, 1)
        grad_raw = (probs * (grad_probs - both(inner_ref, pair))).astype(LOW)
        dv_acc[pl.ds(first, window), lanes] += contract(probs.astype(LOW), grad, 1, 0)
        dk_acc[pl.ds(first, window), lanes] += contract(grad_raw, query, 1, 0)
        grad_query = join_heads(contract(grad_raw, keys, 0, 0)) * SCALE
        dq_ref[:, lanes] = rotate_pair(grad_query, cosine, sine).astype(LOW)

    @pl.when(step == steps - 1)
    def _():
        first_core = layout.core(info) == 0
        for pair in range(pairs):
            lanes = slice(pair * PAIR, (pair + 1) * PAIR)
            dk = rotate_pair(dk_acc[:, lanes], cos_ref[...], -sin_ref[...])
            dv = dv_acc[:, lanes]
            keep_ref[:, lanes] = jnp.where(first_core, dk, dv).astype(LOW)
            send_ref[:, lanes] = jnp.where(first_core, dv, dk).astype(LOW)


def attend_backward(
    layout, info, part, parts, query, keys, values, grads, lse, inner, cosine, sine, *deps
):
    rows, width = query.shape
    halo_steps = (keys.shape[0] - rows) // Q_ROWS
    lanes = width // parts
    info = jnp.concatenate([info, jnp.full((1,), part * lanes // HEAD_DIM, jnp.int32)])

    def cols(array):
        return pl.BlockSpec((array.shape[0], lanes), lambda i: (0, part))

    def whole(array):
        return pl.BlockSpec(array.shape, lambda i: (0, 0))

    block = pl.BlockSpec((Q_ROWS, lanes), lambda i: (i, part))
    stats = pl.BlockSpec((1, *lse.shape[1:]), lambda i: (i, 0, 0))
    own = pl.BlockSpec((Q_ROWS, PAIR), lambda i: (halo_steps + i, 0))
    flat = pl.BlockSpec((keys.shape[0], lanes), lambda i: (0, 0))
    return pl.pallas_call(
        with_deps(functools.partial(attend_backward_kernel, layout), 11, len(deps)),
        out_shape=(
            jax.ShapeDtypeStruct((rows, lanes), LOW),
            jax.ShapeDtypeStruct((keys.shape[0], lanes), LOW),
            jax.ShapeDtypeStruct((keys.shape[0], lanes), LOW),
        ),
        grid=(rows // Q_ROWS,),
        in_specs=[
            pl.BlockSpec(memory_space=pltpu.SMEM), block, cols(keys), cols(values), block,
            stats, stats, whole(cosine), whole(sine), own, own,
        ]
        + [pl.BlockSpec(memory_space=pl.ANY)] * len(deps),
        out_specs=(pl.BlockSpec((Q_ROWS, lanes), lambda i: (i, 0)), flat, flat),
        scratch_shapes=[
            pltpu.VMEM((keys.shape[0], lanes), F32),
            pltpu.VMEM((keys.shape[0], lanes), F32),
        ],
        compiler_params=pltpu.CompilerParams(vmem_limit_bytes=VMEM_LIMIT),
        cost_estimate=COST,
        name="attend_backward",
    )(info, query, keys, values, grads, lse, inner, cosine, sine, cosine, sine, *deps)


def seen_grads_kernel(layout, blocks, parts, *refs):
    info = refs[0]
    seen = refs[1 : 1 + blocks]
    wq_ref, wk_ref, wv_ref, gain_ref = refs[1 + blocks : 5 + blocks]
    at = 5 + blocks
    dqs, keeps, sends = (refs[at + j * parts : at + (j + 1) * parts] for j in range(3))
    far_ref, near_ref, own_ref, dgain_ref = refs[-4:]
    rows = seen[0].shape[0]
    first_core = layout.core(info) == 0
    total = None
    for j, normed in enumerate(seen):
        place = slice(j * rows, (j + 1) * rows)
        keep = jnp.concatenate([ref[place] for ref in keeps], axis=1)
        send = jnp.concatenate([ref[place] for ref in sends], axis=1)
        dk, dv = jnp.where(first_core, keep, send), jnp.where(first_core, send, keep)
        grad = contract(dk, wk_ref[...], 1, 1) + contract(dv, wv_ref[...], 1, 1)
        if j == blocks - 1:
            dq = jnp.concatenate([ref[...] for ref in dqs], axis=1)
            grad = grad + contract(dq, wq_ref[...], 1, 1)
            own_ref[...] = grad
        elif j == 0:
            far_ref[...] = grad.astype(LOW)
        else:
            near_ref[(j - 1) * rows : j * rows] = grad.astype(LOW)
        gained = jnp.sum(grad * normed[...].astype(F32), axis=0, keepdims=True)
        total = gained if total is None else total + gained
    dgain_ref[...] = total / gain_ref[...]


def seen_grads(layout, info, seen, w_q, w_k, w_v, gain, dqs, keeps, sends, *deps):
    rows, width = seen[0].shape
    vmem = pl.BlockSpec(memory_space=pltpu.VMEM)
    args = (*seen, w_q, w_k, w_v, gain, *dqs, *keeps, *sends)
    return pl.pallas_call(
        with_deps(
            functools.partial(seen_grads_kernel, layout, len(seen), len(dqs)),
            1 + len(args), len(deps),
        ),
        out_shape=(
            jax.ShapeDtypeStruct((rows, width), LOW),
            jax.ShapeDtypeStruct((rows * (len(seen) - 2), width), LOW),
            jax.ShapeDtypeStruct((rows, width), F32),
            jax.ShapeDtypeStruct((1, width), F32),
        ),
        in_specs=[pl.BlockSpec(memory_space=pltpu.SMEM)]
        + [vmem] * len(args)
        + [pl.BlockSpec(memory_space=pl.ANY)] * len(deps),
        out_specs=(vmem,) * 4,
        compiler_params=pltpu.CompilerParams(vmem_limit_bytes=VMEM_LIMIT),
        cost_estimate=COST,
        name="seen_grads",
    )(info, *args, *deps)


def attend_grads_kernel(
    layout, info, near_t, far_t, short_t, keep, got, dq, got_dq, heads, got_heads, *refs
):
    outs, held = refs[:-1], refs[-1]
    deep = outs[0].shape[-2]
    wide = outs[0].shape[-1] // 2
    rows = dq.shape[0]
    slots = grad_slots(layout)
    first_core = layout.core(info) == 0
    right_short = jnp.concatenate(
        [
            jnp.where(first_core, query[...], other[...])
            for query, other in ((dq, heads), (got_dq, got_heads))
        ],
        axis=0,
    )
    right_near = jnp.concatenate([keep[rows:], got[rows:]], axis=0)
    right_far = jnp.concatenate([keep[:rows], got[:rows]], axis=0)
    for a in range(layout.n_row):
        place = row_of(layout, info, a, deep)
        grads = (
            contract(short_t[place], right_short, 1, 0),
            contract(near_t[place], right_near, 1, 0) + contract(far_t[place], right_far, 1, 0),
        )
        for j, grad in enumerate(grads):
            grad = grad.astype(LOW)
            for col in range(layout.n_col):
                held[a % 2, col, :, j * wide : (j + 1) * wide] = grad[
                    :, col * wide : (col + 1) * wide
                ]
        for k in range(layout.n_col):
            out, index = slots[a, k]
            col = lax.rem(layout.col(info) + (layout.n_col - k), layout.n_col)
            outs[out][index] = held[a % 2, col]


def attend_grads(
    layout, info, near_t, far_t, short_t, keep, got, dq, got_dq, heads, got_heads, *deps
):
    rows, width = heads.shape
    vmem = pl.BlockSpec(memory_space=pltpu.VMEM)
    deep, lanes = width // layout.n_row, 2 * width // layout.n_col
    shapes = grad_shapes(layout, deep, lanes)
    args = (near_t, far_t, short_t, keep, got, dq, got_dq, heads, got_heads)
    return pl.pallas_call(
        with_deps(functools.partial(attend_grads_kernel, layout), 1 + len(args), len(deps)),
        out_shape=shapes,
        in_specs=[pl.BlockSpec(memory_space=pltpu.SMEM)]
        + [vmem] * len(args)
        + [pl.BlockSpec(memory_space=pl.ANY)] * len(deps),
        out_specs=(vmem,) * len(shapes),
        scratch_shapes=[pltpu.VMEM((2, layout.n_col, deep, lanes), LOW)],
        compiler_params=pltpu.CompilerParams(vmem_limit_bytes=VMEM_LIMIT),
        cost_estimate=COST,
        name="attend_grads",
    )(info, *args, *deps)


def shift(count, by):
    return [(i, (i + by) % count) for i in range(count)]


SWAP = [(0, 1), (1, 0)]


def after(value, *deps):
    return lax.optimization_barrier((value, *deps))[0]


def gather_cols(layout, block):
    n_col = layout.n_col
    return [block] + [lax.ppermute(block, "col", shift(n_col, k)) for k in range(1, n_col)]


def gather_sides(layout, plane):
    if layout.n_row != 4:
        return [plane]
    return [plane] + [
        lax.ppermute(plane, "row", [(i, i ^ by) for i in range(4)]) for by in (1, 2)
    ]


def gather_corner(layout, sides):
    if layout.n_row != 4:
        return [lax.all_gather(sides[0], "row", axis=0, tiled=True)]
    return sides + [lax.ppermute(sides[1], "row", [(i, i ^ 2) for i in range(4)])]


def both_cores(pieces):
    return pieces + [lax.ppermute(piece, "ba", SWAP) for piece in pieces]


def plus(left, right):
    return left.astype(F32) + right.astype(F32)


def scatter_start(layout, grads):
    if layout.n_row != 4:
        return (lax.psum_scatter(grads[0], "row", scatter_dimension=0, tiled=True)[0],)
    _, for_x, for_y, _, _ = grads
    return (
        lax.ppermute(for_x, "row", [(i, i ^ 1) for i in range(4)]),
        lax.ppermute(for_y, "row", [(i, i ^ 2) for i in range(4)]),
    )


def scatter_next(layout, grads, got):
    if layout.n_row != 4:
        return got
    got_x, got_y = got
    _, _, _, on_y, on_x = grads
    return (
        plus(on_y, got_x[1]).astype(LOW),
        plus(on_x, got_y[1]).astype(LOW),
    )


def scatter_cross(layout, sums):
    if layout.n_row != 4:
        return sums
    return (
        lax.ppermute(sums[0], "row", [(i, i ^ 2) for i in range(4)]),
        lax.ppermute(sums[1], "row", [(i, i ^ 1) for i in range(4)]),
    )


def scatter_plane(layout, grads, got, crossed):
    if layout.n_row != 4:
        return list(crossed[0])
    from_y, from_x = crossed
    cut = layout.n_col // 2
    own = grads[0]
    return [
        (plus(own[k], got[0][0, k]) + from_y[k].astype(F32)).astype(LOW)
        if k < cut
        else (plus(own[k], got[1][0, k - cut]) + from_x[k - cut].astype(F32)).astype(LOW)
        for k in range(layout.n_col)
    ]


def scatter_cols(layout, plane):
    n_col = layout.n_col
    return [plane[0]] + [
        lax.ppermute(plane[k], "col", shift(n_col, n_col - k)) for k in range(1, n_col)
    ]


def add_up(blocks):
    total = blocks[0].astype(F32)
    for block in blocks[1:]:
        total = total + block.astype(F32)
    return total


def xor_sum(values, axis, size, bits):
    for bit in bits:
        values = values + lax.ppermute(values, axis, [(i, i ^ (1 << bit)) for i in range(size)])
    return values


def shards(
    n_row, n_col, tokens, lengths, w_query, w_key, w_value, w_out, w_gate, w_up, w_down,
    gain_attn, gain_mlp, cotangent,
):
    rows, width = tokens.shape
    core, row, col = lax.axis_index("ba"), lax.axis_index("row"), lax.axis_index("col")
    layout = Layout(n_row, n_col, lengths.shape[1])
    hops = -(-(LONGEST - 1) // rows)
    halo = hops * rows
    step_right = [(i, i + 1) for i in range(n_col - 1)]
    step_left = [(i + 1, i) for i in range(n_col - 1)]

    first_core = core == 0
    half_units = w_down.shape[0] // 2
    w_down_t = w_down.T
    attn_block = jnp.where(
        first_core,
        jnp.concatenate([w_query, w_key], axis=1),
        jnp.concatenate([w_value, w_out.T], axis=1),
    )
    lower, upper = slice(0, half_units), slice(half_units, None)
    mlp_block = jnp.concatenate(
        [
            jnp.where(first_core, weight[:, lower], weight[:, upper])
            for weight in (w_gate, w_up, w_down_t)
        ],
        axis=1,
    )
    first = col * rows
    flip = row if n_row == 4 else jnp.int32(0)
    info = jnp.concatenate([lengths[0], jnp.stack([first, core, flip, col])]).astype(jnp.int32)
    place = first - halo + jnp.arange(halo + rows, dtype=jnp.int32)
    seq_list = [lengths[0, j] for j in range(lengths.shape[1])]
    position = (place - seq_starts(seq_list, place)).astype(F32)
    half = HEAD_DIM // 2
    lane = jnp.arange(PAIR)
    frequency = ROPE_BASE ** (-(lane % half).astype(F32) / half)
    angles = position[:, None] * frequency[None, :]
    cosine = jnp.cos(angles)
    sine = jnp.sin(angles) * jnp.where(lane % HEAD_DIM < half, -1.0, 1.0)[None, :]

    attn_cols = gather_cols(layout, attn_block)
    normed = norm(tokens, gain_attn[None])
    dy_other = lax.ppermute(cotangent, "ba", SWAP)
    dy_t, = turn([[cotangent, dy_other]])
    mlp_cols = gather_cols(layout, after(mlp_block, normed, *attn_cols))
    attn_rows = gather_corner(layout, gather_sides(layout, jnp.stack(attn_cols)))
    seen = [normed]
    for hop in range(hops):
        sent = after(seen[0], dy_t, cosine, sine, *mlp_cols) if hop == 0 else seen[0]
        seen.insert(0, lax.ppermute(sent, "col", step_right))
    mlp_plane = after(jnp.stack(mlp_cols), *attn_rows)
    attn_pieces = both_cores(attn_rows)
    mlp_sides = gather_sides(layout, mlp_plane)

    w_q, w_k, w_v, w_o_t, q, k_near, v_near = prepare(
        layout, info, seen[1:], cosine[rows:], sine[rows:], attn_pieces
    )
    seen_other = [lax.ppermute(block, "ba", SWAP) for block in seen]
    near_t, = turn([[*seen[1:], *seen_other[1:]]], q)
    mlp_pieces = gather_corner(layout, after(mlp_sides, near_t))
    k, v, heads, middle, h2, lse = front(
        layout, info, seen[0], cosine[:rows], sine[:rows], tokens, gain_mlp[None], q, k_near,
        v_near, w_k, w_v, w_o_t, near_t,
    )
    heads_other = lax.ppermute(heads, "ba", SWAP)
    h2_other = lax.ppermute(h2, "ba", SWAP)
    own_out, own_back, send, hidden, d_gate, d_up = mlp(
        layout, info, h2, h2_other, cotangent, dy_other, mlp_pieces
    )
    got = lax.ppermute(send, "ba", SWAP)
    grads_mlp = mlp_grads(
        layout, info, hidden, d_gate, d_up, h2, h2_other, dy_t
    )
    got_mlp = scatter_start(layout, grads_mlp)
    layer_out, d_middle, dm, d_heads, dgain_mlp, inner = middle_grads(
        middle, cotangent, gain_mlp[None], w_o_t, heads, own_out, own_back, got, grads_mlp[0]
    )
    dm_other = lax.ppermute(dm, "ba", SWAP)
    dq, keep_long, send_long = attend_backward(
        layout, info, 0, 1, q, k, v, d_heads, lse, inner, cosine, sine, heads_other, seen_other[0]
    )
    sums_mlp = scatter_next(layout, grads_mlp, after(got_mlp, dq))
    got_long = lax.ppermute(send_long, "ba", SWAP)
    dq_other = lax.ppermute(dq, "ba", SWAP)
    crossed_mlp = scatter_cross(layout, sums_mlp)
    far_t, short_t = turn_rest(
        layout, info, seen[0], seen_other[0], dm, dm_other, near_t, *sums_mlp
    )
    far, near, own, dgain_attn = seen_grads(
        layout, info, seen, w_q, w_k, w_v, gain_attn[None], [dq], [keep_long], [send_long],
        far_t,
    )
    gains = jnp.concatenate([dgain_attn, dgain_mlp])
    gains = gains + lax.ppermute(gains, "ba", SWAP)
    plane_mlp = jnp.stack(scatter_plane(layout, grads_mlp, got_mlp, after(crossed_mlp, far)))
    grads_attn = attend_grads(
        layout, info, near_t, far_t, short_t, keep_long, got_long, dq, dq_other, heads,
        heads_other, gains, plane_mlp,
    )
    blocks_mlp = lax.all_to_all(plane_mlp, "col", 0, 0, tiled=True)
    got_attn = scatter_start(layout, grads_attn)
    arrived = lax.ppermute(far, "col", step_left)
    travelling = near
    for hop in range(1, hops):
        travelling = plus(near[(hop - 1) * rows : hop * rows], arrived).astype(LOW)
        arrived = lax.ppermute(travelling, "col", step_left)
    half_bits = (n_row.bit_length() - 1) // 2
    gains = xor_sum(after(gains, grads_attn[0]), "row", n_row, range(half_bits))
    sums_attn = scatter_next(layout, grads_attn, after(got_attn, travelling, gains))
    crossed_attn = scatter_cross(layout, sums_attn)
    gains = xor_sum(
        after(gains, *sums_attn), "row", n_row, range(half_bits, n_row.bit_length() - 1)
    )
    plane_attn = scatter_plane(layout, grads_attn, got_attn, after(crossed_attn, gains))
    blocks_attn = scatter_cols(layout, plane_attn)
    d_h1 = own + after(arrived, *plane_attn).astype(F32)
    blocks_mlp = after(blocks_mlp, *plane_attn)
    part = add_up([blocks_mlp[k] for k in range(n_col)])
    x = tokens.astype(F32)
    scale = lax.rsqrt(jnp.mean(x * x, axis=1, keepdims=True) + EPSILON)
    weighted = d_h1 * gain_attn[None, :]
    inner = jnp.mean(weighted * x, axis=1, keepdims=True)
    input_grad = (d_middle + scale * weighted - x * (scale**3 * inner)).astype(LOW)
    gains = xor_sum(after(gains, *plane_attn), "col", n_col, range(1))
    part_attn = add_up(after(blocks_attn, input_grad, part, gains))
    gains = xor_sum(gains, "col", n_col, range(1, n_col.bit_length() - 1))

    other_attn = lax.ppermute(part_attn, "ba", SWAP)
    zero_side = jnp.where(first_core, part_attn, other_attn)
    one_side = jnp.where(first_core, other_attn, part_attn)
    wide = width // n_col
    other = lax.ppermute(part, "ba", SWAP)
    cut = part.shape[1] // 3

    def whole(j):
        mine, theirs = part[:, j * cut : (j + 1) * cut], other[:, j * cut : (j + 1) * cut]
        return jnp.concatenate(
            [jnp.where(first_core, mine, theirs), jnp.where(first_core, theirs, mine)], axis=1
        )

    return (
        layer_out, input_grad, zero_side[:, :wide], zero_side[:, wide:], one_side[:, wide:],
        one_side[:, :wide].T, whole(1), whole(2), whole(0).T, gains[0], gains[1],
    )


def solution(mesh):
    tokens = P(("ba", "row", "col"), None)
    in_side, out_side = P("row", "col"), P("col", "row")
    in_specs = (
        tokens, P(("ba", "row"), None), in_side, in_side, in_side, out_side, in_side, in_side,
        out_side, P(), P(), tokens,
    )
    out_specs = (
        tokens, tokens, in_side, in_side, in_side, out_side, in_side, in_side, out_side, P(), P(),
    )
    body = functools.partial(shards, mesh.shape["row"], mesh.shape["col"])
    return jax.shard_map(
        body, mesh=mesh, in_specs=in_specs, out_specs=out_specs, check_vma=False
    )
```

profile of v0, /device:TPU:0, one launch (start us, length us, event | category | flops | bytes accessed | tf_op | source)
XLA Modules:
  0.0 277.8 jit_solution(13486796852065508168)
XLA Ops:
  2.9 3.1 %collective-permute-start.1 = (bf16[192,384]{1,0:T(8,128)(2,1)S(1)}, bf16[192,384]{1,0:T(8,128)(2,1)S(1)}, u32[]{:S(2)}, u32[]{:S(2)}) collective-permute-start(bf16[192,384]{1,0:T(8,128)(2,1)S(1)} %maximum_select_fusion), channel_id=1, source_target_pairs={{0,1},{1,2},{2,3},{3,0},{4,5},{5,6},{6,7},{7,4},{8,9},{9,10},{10,1... | collective-permute-start | bytes 442376 | tf_op jit(solution)/shard_map/ppermute | solution.py:784
  13.9 4.4 %collective-permute-done.2 = bf16[192,384]{1,0:T(8,128)(2,1)S(1)} collective-permute-done((bf16[192,384]{1,0:T(8,128)(2,1)S(1)}, bf16[192,384]{1,0:T(8,128)(2,1)S(1)}, u32[]{:S(2)}, u32[]{:S(2)}) %collective-permute-start.2) | collective-permute-done | bytes 147488 | tf_op jit(solution)/shard_map/ppermute | solution.py:784
  20.0 3.7 %collective-permute-start.4 = (bf16[192,768]{1,0:T(8,128)(2,1)S(1)}, bf16[192,768]{1,0:T(8,128)(2,1)S(1)}, u32[]{:S(2)}, u32[]{:S(2)}) collective-permute-start(bf16[192,768]{1,0:T(8,128)(2,1)S(1)} %pad_maximum_fusion.5), channel_id=1, source_target_pairs={{0,1},{1,2},{2,3},{3,0},{4,5},{5,6},{6,7},{7,4},{8,9},{9,10},{10,1... | collective-permute-start | bytes 884744 | tf_op jit(solution)/shard_map/ppermute | solution.py:784
  34.2 9.1 %collective-permute-done.5 = bf16[192,768]{1,0:T(8,128)(2,1)S(1)} collective-permute-done((bf16[192,768]{1,0:T(8,128)(2,1)S(1)}, bf16[192,768]{1,0:T(8,128)(2,1)S(1)}, u32[]{:S(2)}, u32[]{:S(2)}) %collective-permute-start.5) | collective-permute-done | bytes 294944 | tf_op jit(solution)/shard_map/ppermute | solution.py:784
  51.8 7.6 %collective-permute-start.7 = (bf16[384,768]{1,0:T(8,128)(2,1)S(1)}, bf16[384,768]{1,0:T(8,128)(2,1)S(1)}, u32[]{:S(2)}, u32[]{:S(2)}) collective-permute-start(bf16[384,768]{1,0:T(8,128)(2,1)S(1)} %copy-done.3), channel_id=1, source_target_pairs={{0,1},{1,2},{2,3},{4,5},{5,6},{6,7},{8,9},{9,10},{10,11},{12,13},{... | collective-permute-start | bytes 1769480 | tf_op jit(solution)/shard_map/ppermute | solution.py:923
  61.5 11.0 %collective-permute-done.7.refs_1_.refs_0_.refs_2_ = bf16[384,768]{1,0:T(8,128)(2,1)S(1)} collective-permute-done((bf16[384,768]{1,0:T(8,128)(2,1)S(1)}, bf16[384,768]{1,0:T(8,128)(2,1)S(1)}, u32[]{:S(2)}, u32[]{:S(2)}) %collective-permute-start.7) | collective-permute-done | bytes 589856 | tf_op jit(solution)/shard_map/ppermute | solution.py:923
  76.0 4.6 %collective-permute-start.8 = (bf16[384,768]{1,0:T(8,128)(2,1)S(1)}, bf16[384,768]{1,0:T(8,128)(2,1)S(1)}, u32[]{:S(2)}, u32[]{:S(2)}) collective-permute-start(bf16[384,768]{1,0:T(8,128)(2,1)S(1)} %collective-permute-done.7.refs_1_.refs_0_.refs_2_), channel_id=1, source_target_pairs={{0,1},{1,2},{2,3},{4,5},{5,6},{6,7},{8,9},{9,10},{10,11},{12,13},{... | collective-permute-start | bytes 1769480 | tf_op jit(solution)/shard_map/ppermute | solution.py:923
  80.7 9.1 %prepare.1 = (bf16[768,768]{1,0:T(8,128)(2,1)}, bf16[768,768]{1,0:T(8,128)(2,1)}, bf16[768,768]{1,0:T(8,128)(2,1)}, bf16[768,768]{1,0:T(8,128)(2,1)}, bf16[384,7...) custom-call(s32[8]{0:T(128)} %concatenate.54.refs_0_, bf16[384,768]{1,0:T(8,128)(2,1)} %copy-done.6, ...), custom_call_target="tpu_custom_call" | custom-call | flops 1000 | bytes 1000 | tf_op jit(solution)/shard_map/prepare/pallas_call | solution.py:191
  89.8 3.7 %turn.3.refs_12_.refs_5_.refs_1_ = bf16[768,1536]{1,0:T(8,128)(2,1)} custom-call(bf16[384,768]{1,0:T(8,128)(2,1)} %copy-done.6, bf16[384,768]{1,0:T(8,128)(2,1)} %norm.1.refs_2_.refs_1_.refs_3_, bf16[384,768]{1,0:T(8,128)(2,1)} %collective-permute-done.16.refs_2_, bf16[384,768]{1,0:T(8,128)(2,1)} %collective-permute-done.17.refs_3_, ...), custom_call_target="tpu_custom_call" | custom-call | flops 1000 | bytes 1000 | tf_op jit(solution)/shard_map/turn/pallas_call | solution.py:519
  96.8 16.4 %front.1 = (bf16[1152,768]{1,0:T(8,128)(2,1)}, bf16[1152,768]{1,0:T(8,128)(2,1)}, bf16[384,768]{1,0:T(8,128)(2,1)}, f32[384,768]{1,0:T(8,128)}, bf16[384,768]{1,0:T(8,128)(2,1)}, /*index=5*/f32[3,16,128]{2,1,0:T(8,128)}) custom-call(s32[8]{0:T(128)} %concatenate.54.refs_0_, bf16[384,768]{1,0:T(8,128)(2,1)} %copy-done.4, f32[384,128]{1,0:T(8,128)} %slice.234.refs_2_, ...), custom_call_target="tpu_custom_call" | custom-call | flops 1000 | bytes 1000 | tf_op jit(solution)/shard_map/front/pallas_call | solution.py:276
  115.5 5.9 %collective-permute-done.21.refs_8_ = bf16[4,192,768]{2,1,0:T(8,128)(2,1)S(1)} collective-permute-done((bf16[4,192,768]{2,1,0:T(8,128)(2,1)}, bf16[4,192,768]{2,1,0:T(8,128)(2,1)S(1)}, u32[]{:S(2)}, u32[]{:S(2)}) %collective-permute-start.21) | collective-permute-done | bytes 1179680 | tf_op jit(solution)/shard_map/ppermute | solution.py:798
  122.5 15.6 %mlp.1 = (f32[384,768]{1,0:T(8,128)}, f32[384,768]{1,0:T(8,128)}, bf16[2,384,768]{2,1,0:T(8,128)(2,1)}, bf16[768,1024]{1,0:T(8,128)(2,1)}, bf16[768,1024]{1,0:T(8,128)(2,1)}, /*index=5*/bf16[768,1024]{1,0:T(8,128)(2,1)}) custom-call(s32[8]{0:T(128)} %concatenate.54.refs_0_, bf16[384,768]{1,0:T(8,128)(2,1)} %get-tuple-element.88.refs_1_.refs_4_, ...), custom_call_target="tpu_custom_call" | custom-call | flops 1000 | bytes 1000 | tf_op jit(solution)/shard_map/mlp/pallas_call | solution.py:360
  138.2 9.2 %mlp_grads.1 = (bf16[4,192,768]{2,1,0:T(8,128)(2,1)}, bf16[2,2,192,768]{3,2,1,0:T(8,128)(2,1)}, bf16[2,2,192,768]{3,2,1,0:T(8,128)(2,1)}, bf16[2,192,768]{2,1,0:T(8,128)(2,1)}, bf16[2,192,768]{2,1,0:T(8,128)(2,1)}) custom-call(s32[8]{0:T(128)} %concatenate.54.refs_0_, bf16[768,1024]{1,0:T(8,128)(2,1)} %get-tuple-element.96.refs_1_, ...), custom_call_target="tpu_custom_call" | custom-call | flops 1000 | bytes 1000 | tf_op jit(solution)/shard_map/mlp_grads/pallas_call | solution.py:483
  149.6 6.0 %middle_grads.1 = (bf16[384,768]{1,0:T(8,128)(2,1)}, f32[384,768]{1,0:T(8,128)}, bf16[384,768]{1,0:T(8,128)(2,1)}, bf16[384,768]{1,0:T(8,128)(2,1)}, f32[1,768]{1,0:T(1,128)}, /*index=5*/f32[3,16,128]{2,1,0:T(8,128)}) custom-call(f32[384,768]{1,0:T(8,128)} %get-tuple-element.86.refs_0_, bf16[384,768]{1,0:T(8,128)(2,1)} %refs_1_.1, ...), custom_call_target="tpu_custom_call" | custom-call | flops 1000 | bytes 1000 | tf_op jit(solution)/shard_map/middle_grads/pallas_call | solution.py:413
  156.6 19.4 %attend_backward.1 = (bf16[384,768]{1,0:T(8,128)(2,1)}, bf16[1152,768]{1,0:T(8,128)(2,1)}, bf16[1152,768]{1,0:T(8,128)(2,1)}) custom-call(s32[9]{0:T(128)} %concatenate.64.refs_0_, bf16[384,768]{1,0:T(8,128)(2,1)} %get-tuple-element.80.refs_4_.refs_6_.refs_1_, bf16[1152,768]{1,0:T(8,128)(2,1)} %get-tuple-element.103.refs_2_, ...), custom_call_target="tpu_custom_call" | custom-call | flops 1000 | bytes 1000 | tf_op jit(solution)/shard_map/attend_backward/pallas_call | solution.py:635
  183.1 4.5 %turn_rest.1 = (bf16[768,768]{1,0:T(8,128)(2,1)}, bf16[768,768]{1,0:T(8,128)(2,1)}) custom-call(s32[8]{0:T(128)} %concatenate.54.refs_0_, bf16[384,768]{1,0:T(8,128)(2,1)} %copy-done.4, bf16[384,768]{1,0:T(8,128)(2,1)} %copy-done.12, bf16[384,768]{1,0:T(8,128)(2,1)} %get-tuple-element.111.refs_3_, bf16[384,768]{1,0:T(8,128)(2,1)} %copy-done.22, ...), custom_call_target="tpu_custom_call" | custom-call | flops 1000 | bytes 1000 | tf_op jit(solution)/shard_map/turn_rest/pallas_call | solution.py:553
  187.5 8.3 %seen_grads.1 = (bf16[384,768]{1,0:T(8,128)(2,1)}, bf16[384,768]{1,0:T(8,128)(2,1)}, f32[384,768]{1,0:T(8,128)}, f32[1,768]{1,0:T(1,128)}) custom-call(s32[8]{0:T(128)} %concatenate.54.refs_0_, bf16[384,768]{1,0:T(8,128)(2,1)} %copy-done.4, bf16[384,768]{1,0:T(8,128)(2,1)} %copy-done.6, bf16[384,768]{1,0:T(8,128)(2,1)} %norm.1.refs_2_.refs_1_.refs_3_, ...), custom_call_target="tpu_custom_call" | custom-call | flops 1000 | bytes 1000 | tf_op jit(solution)/shard_map/seen_grads/pallas_call | solution.py:692
  202.0 7.4 %all-to-all-start = ((bf16[4,192,768]{2,1,0:T(8,128)(2,1)}), bf16[4,192,768]{2,1,0:T(8,128)(2,1)S(1)}, u32[]{:S(2)}, u32[]{:S(2)}) async-start(bf16[4,192,768]{2,1,0:T(8,128)(2,1)} %pad_maximum_fusion.1.refs_11_), calls=%async_computation | async-start | bytes 2359296 | tf_op jit(solution)/shard_map/all_to_all | solution.py:973
  212.0 9.3 %attend_grads.1 = (bf16[4,192,384]{2,1,0:T(8,128)(2,1)}, bf16[2,2,192,384]{3,2,1,0:T(8,128)(2,1)}, bf16[2,2,192,384]{3,2,1,0:T(8,128)(2,1)}, bf16[2,192,384]{2,1,0:T(8,128)(2,1)}, bf16[2,192,384]{2,1,0:T(8,128)(2,1)}) custom-call(s32[8]{0:T(128)} %concatenate.54.refs_0_, bf16[768,1536]{1,0:T(8,128)(2,1)} %turn.3.refs_12_.refs_5_.refs_1_, ...), custom_call_target="tpu_custom_call" | custom-call | flops 1000 | bytes 1000 | tf_op jit(solution)/shard_map/attend_grads/pallas_call | solution.py:757
  227.6 9.1 %collective-permute-done.37 = f32[2,768]{1,0:T(2,128)S(1)} collective-permute-done((f32[2,768]{1,0:T(2,128)S(1)}, f32[2,768]{1,0:T(2,128)S(1)}, u32[]{:S(2)}, u32[]{:S(2)}) %collective-permute-start.37) | collective-permute-done | bytes 6176 | tf_op jit(solution)/shard_map/ppermute | solution.py:869
  240.6 5.3 %collective-permute-done.40 = f32[2,768]{1,0:T(2,128)S(1)} collective-permute-done((f32[2,768]{1,0:T(2,128)S(1)}, f32[2,768]{1,0:T(2,128)S(1)}, u32[]{:S(2)}, u32[]{:S(2)}) %collective-permute-start.40) | collective-permute-done | bytes 6176 | tf_op jit(solution)/shard_map/ppermute | solution.py:869
  246.9 3.3 %collective-permute-start.41 = (bf16[192,384]{1,0:T(8,128)(2,1)}, bf16[192,384]{1,0:T(8,128)(2,1)}, u32[]{:S(2)}, u32[]{:S(2)}) collective-permute-start(bf16[192,384]{1,0:T(8,128)(2,1)} %get-tuple-element.179), channel_id=1, source_target_pairs={{0,3},{1,0},{2,1},{3,2},{4,7},{5,4},{6,5},{7,6},{8,11},{9,8},{10,9... | collective-permute-start | bytes 442376 | tf_op jit(solution)/shard_map/ppermute | solution.py:856
  258.0 8.2 %collective-permute-done.42 = bf16[192,384]{1,0:T(8,128)(2,1)} collective-permute-done((bf16[192,384]{1,0:T(8,128)(2,1)}, bf16[192,384]{1,0:T(8,128)(2,1)}, u32[]{:S(2)}, u32[]{:S(2)}) %collective-permute-start.42) | collective-permute-done | bytes 147488 | tf_op jit(solution)/shard_map/ppermute | solution.py:856
  267.8 4.2 %collective-permute-done.47 = f32[2,768]{1,0:T(2,128)S(1)} collective-permute-done((f32[2,768]{1,0:T(2,128)S(1)}, f32[2,768]{1,0:T(2,128)S(1)}, u32[]{:S(2)}, u32[]{:S(2)}) %collective-permute-start.47) | collective-permute-done | bytes 6176 | tf_op jit(solution)/shard_map/ppermute | solution.py:869
  (222 shorter events, 85.5 us)
Async XLA Ops:
  9.9 38.5 %collective-permute-start = (bf16[384,768]{1,0:T(8,128)(2,1)}, bf16[384,768]{1,0:T(8,128)(2,1)S(1)}, u32[]{:S(2)}, u32[]{:S(2)}) collective-permute-start(bf16[384,768]{1,0:T(8,128)(2,1)} %refs_1_.1), channel_id=1, source_target_pairs={{0,16},{16,0},{1,17},{17,1},{2,18},{18,2},{3,19},{19,3},{4,20},{20... | collective-permute-start | bytes 1769480 | tf_op jit(solution)/shard_map/ppermute | solution.py:916
  18.4 25.0 %collective-permute-start.9 = (bf16[4,192,384]{2,1,0:T(8,128)(2,1)S(1)}, bf16[4,192,384]{2,1,0:T(8,128)(2,1)}, u32[]{:S(2)}, u32[]{:S(2)}) collective-permute-start(bf16[4,192,384]{2,1,0:T(8,128)(2,1)S(1)} %pad_maximum_fusion.2.refs_5_), channel_id=1, source_target_pairs={{0,4},{4,0},{8,12},{12,8},{1,5},{5,1},{9,13},{13,9},{2,6},{6,2},{1... | collective-permute-start | bytes 1769480 | tf_op jit(solution)/shard_map/ppermute | solution.py:791
  23.6 19.7 %collective-permute-start.5 = (bf16[192,768]{1,0:T(8,128)(2,1)S(1)}, bf16[192,768]{1,0:T(8,128)(2,1)S(1)}, u32[]{:S(2)}, u32[]{:S(2)}) collective-permute-start(bf16[192,768]{1,0:T(8,128)(2,1)S(1)} %pad_maximum_fusion.5), channel_id=1, source_target_pairs={{0,2},{1,3},{2,0},{3,1},{4,6},{5,7},{6,4},{7,5},{8,10},{9,11},{10,... | collective-permute-start | bytes 884744 | tf_op jit(solution)/shard_map/ppermute | solution.py:784
  29.1 17.9 %collective-permute-start.6 = (bf16[192,768]{1,0:T(8,128)(2,1)S(1)}, bf16[192,768]{1,0:T(8,128)(2,1)S(1)}, u32[]{:S(2)}, u32[]{:S(2)}) collective-permute-start(bf16[192,768]{1,0:T(8,128)(2,1)S(1)} %pad_maximum_fusion.5), channel_id=1, source_target_pairs={{0,3},{1,0},{2,1},{3,2},{4,7},{5,4},{6,5},{7,6},{8,11},{9,8},{10,9... | collective-permute-start | bytes 884744 | tf_op jit(solution)/shard_map/ppermute | solution.py:784
  32.7 26.9 %collective-permute-start.10 = (bf16[4,192,384]{2,1,0:T(8,128)(2,1)S(1)}, bf16[4,192,384]{2,1,0:T(8,128)(2,1)S(1)}, u32[]{:S(2)}, u32[]{:S(2)}) collective-permute-start(bf16[4,192,384]{2,1,0:T(8,128)(2,1)S(1)} %pad_maximum_fusion.2.refs_5_), channel_id=1, source_target_pairs={{0,8},{4,12},{8,0},{12,4},{1,9},{5,13},{9,1},{13,5},{2,10},{6,14},... | collective-permute-start | bytes 1769480 | tf_op jit(solution)/shard_map/ppermute | solution.py:791
  43.3 17.3 %collective-permute-start.12 = (bf16[4,192,384]{2,1,0:T(8,128)(2,1)S(1)}, bf16[4,192,384]{2,1,0:T(8,128)(2,1)S(1)}, u32[]{:S(2)}, u32[]{:S(2)}) collective-permute-start(bf16[4,192,384]{2,1,0:T(8,128)(2,1)S(1)} %pad_maximum_fusion.2.refs_5_), channel_id=1, source_target_pairs={{0,16},{16,0},{1,17},{17,1},{2,18},{18,2},{3,19},{19,3},{4,20},{20... | collective-permute-start | bytes 1769480 | tf_op jit(solution)/shard_map/ppermute | solution.py:802
  43.3 16.7 %collective-permute-start.11 = (bf16[4,192,384]{2,1,0:T(8,128)(2,1)}, bf16[4,192,384]{2,1,0:T(8,128)(2,1)}, u32[]{:S(2)}, u32[]{:S(2)}) collective-permute-start(bf16[4,192,384]{2,1,0:T(8,128)(2,1)} %collective-permute-done.9.refs_6_), channel_id=1, source_target_pairs={{0,8},{4,12},{8,0},{12,4},{1,9},{5,13},{9,1},{13,5},{2,10},{6,14},... | collective-permute-start | bytes 1769480 | tf_op jit(solution)/shard_map/ppermute | solution.py:798
  51.8 20.6 %collective-permute-start.7 = (bf16[384,768]{1,0:T(8,128)(2,1)S(1)}, bf16[384,768]{1,0:T(8,128)(2,1)S(1)}, u32[]{:S(2)}, u32[]{:S(2)}) collective-permute-start(bf16[384,768]{1,0:T(8,128)(2,1)S(1)} %copy-done.3), channel_id=1, source_target_pairs={{0,1},{1,2},{2,3},{4,5},{5,6},{6,7},{8,9},{9,10},{10,11},{12,13},{... | collective-permute-start | bytes 1769480 | tf_op jit(solution)/shard_map/ppermute | solution.py:923
  60.1 33.4 %collective-permute-start.19 = (bf16[4,192,768]{2,1,0:T(8,128)(2,1)}, bf16[4,192,768]{2,1,0:T(8,128)(2,1)}, u32[]{:S(2)}, u32[]{:S(2)}) collective-permute-start(bf16[4,192,768]{2,1,0:T(8,128)(2,1)} %pad_maximum_fusion.refs_5_), channel_id=1, source_target_pairs={{0,4},{4,0},{8,12},{12,8},{1,5},{5,1},{9,13},{13,9},{2,6},{6,2},{1... | collective-permute-start | bytes 3538952 | tf_op jit(solution)/shard_map/ppermute | solution.py:791
  60.6 32.8 %collective-permute-start.20 = (bf16[4,192,768]{2,1,0:T(8,128)(2,1)}, bf16[4,192,768]{2,1,0:T(8,128)(2,1)}, u32[]{:S(2)}, u32[]{:S(2)}) collective-permute-start(bf16[4,192,768]{2,1,0:T(8,128)(2,1)} %pad_maximum_fusion.refs_5_), channel_id=1, source_target_pairs={{0,8},{4,12},{8,0},{12,4},{1,9},{5,13},{9,1},{13,5},{2,10},{6,14},... | collective-permute-start | bytes 3538952 | tf_op jit(solution)/shard_map/ppermute | solution.py:791
  72.4 17.3 %collective-permute-start.17 = (bf16[384,768]{1,0:T(8,128)(2,1)S(1)}, bf16[384,768]{1,0:T(8,128)(2,1)}, u32[]{:S(2)}, u32[]{:S(2)}) collective-permute-start(bf16[384,768]{1,0:T(8,128)(2,1)S(1)} %copy-done.3), channel_id=1, source_target_pairs={{0,16},{16,0},{1,17},{17,1},{2,18},{18,2},{3,19},{19,3},{4,20},{20... | collective-permute-start | bytes 1769480 | tf_op jit(solution)/shard_map/ppermute | solution.py:931
  73.0 16.8 %collective-permute-start.16 = (bf16[384,768]{1,0:T(8,128)(2,1)S(1)}, bf16[384,768]{1,0:T(8,128)(2,1)}, u32[]{:S(2)}, u32[]{:S(2)}) collective-permute-start(bf16[384,768]{1,0:T(8,128)(2,1)S(1)} %collective-permute-done.7.refs_1_.refs_0_.refs_2_), channel_id=1, source_target_pairs={{0,16},{16,0},{1,17},{17,1},{2,18},{18,2},{3,19},{19,3},{4,20},{20... | collective-permute-start | bytes 1769480 | tf_op jit(solution)/shard_map/ppermute | solution.py:931
  76.0 20.0 %collective-permute-start.8 = (bf16[384,768]{1,0:T(8,128)(2,1)S(1)}, bf16[384,768]{1,0:T(8,128)(2,1)S(1)}, u32[]{:S(2)}, u32[]{:S(2)}) collective-permute-start(bf16[384,768]{1,0:T(8,128)(2,1)S(1)} %collective-permute-done.7.refs_1_.refs_0_.refs_2_), channel_id=1, source_target_pairs={{0,1},{1,2},{2,3},{4,5},{5,6},{6,7},{8,9},{9,10},{10,11},{12,13},{... | collective-permute-start | bytes 1769480 | tf_op jit(solution)/shard_map/ppermute | solution.py:923
  93.4 28.0 %collective-permute-start.21 = (bf16[4,192,768]{2,1,0:T(8,128)(2,1)}, bf16[4,192,768]{2,1,0:T(8,128)(2,1)S(1)}, u32[]{:S(2)}, u32[]{:S(2)}) collective-permute-start(bf16[4,192,768]{2,1,0:T(8,128)(2,1)} %collective-permute-done.19.refs_6_), channel_id=1, source_target_pairs={{0,8},{4,12},{8,0},{12,4},{1,9},{5,13},{9,1},{13,5},{2,10},{6,14},... | collective-permute-start | bytes 3538952 | tf_op jit(solution)/shard_map/ppermute | solution.py:798
  147.4 28.7 %collective-permute-start.26 = (bf16[2,2,192,768]{3,2,1,0:T(8,128)(2,1)}, bf16[2,2,192,768]{3,2,1,0:T(8,128)(2,1)}, u32[]{:S(2)}, u32[]{:S(2)}) collective-permute-start(bf16[2,2,192,768]{3,2,1,0:T(8,128)(2,1)} %get-tuple-element.113), channel_id=1, source_target_pairs={{0,4},{4,0},{8,12},{12,8},{1,5},{5,1},{9,13},{13,9},{2,6},{6,2},{1... | collective-permute-start | bytes 3538952 | tf_op jit(solution)/shard_map/ppermute | solution.py:814
  148.0 28.4 %collective-permute-start.27 = (bf16[2,2,192,768]{3,2,1,0:T(8,128)(2,1)}, bf16[2,2,192,768]{3,2,1,0:T(8,128)(2,1)}, u32[]{:S(2)}, u32[]{:S(2)}) collective-permute-start(bf16[2,2,192,768]{3,2,1,0:T(8,128)(2,1)} %get-tuple-element.114), channel_id=1, source_target_pairs={{0,8},{4,12},{8,0},{12,4},{1,9},{5,13},{9,1},{13,5},{2,10},{6,14},... | collective-permute-start | bytes 3538952 | tf_op jit(solution)/shard_map/ppermute | solution.py:815
  176.3 34.4 %collective-permute-start.30 = (bf16[1152,768]{1,0:T(8,128)(2,1)}, bf16[1152,768]{1,0:T(8,128)(2,1)S(1)}, u32[]{:S(2)}, u32[]{:S(2)}) collective-permute-start(bf16[1152,768]{1,0:T(8,128)(2,1)} %get-tuple-element.110.refs_10_), channel_id=1, source_target_pairs={{0,16},{16,0},{1,17},{17,1},{2,18},{18,2},{3,19},{19,3},{4,20},{20... | collective-permute-start | bytes 5308424 | tf_op jit(solution)/shard_map/ppermute | solution.py:956
  178.1 19.0 %collective-permute-start.34 = (bf16[2,192,768]{2,1,0:T(8,128)(2,1)S(1)}, bf16[2,192,768]{2,1,0:T(8,128)(2,1)S(1)}, u32[]{:S(2)}, u32[]{:S(2)}) collective-permute-start(bf16[2,192,768]{2,1,0:T(8,128)(2,1)S(1)} %fusion.4.refs_7_), channel_id=1, source_target_pairs={{0,4},{4,0},{8,12},{12,8},{1,5},{5,1},{9,13},{13,9},{2,6},{6,2},{1... | collective-permute-start | bytes 1769480 | tf_op jit(solution)/shard_map/ppermute | solution.py:835
  180.8 16.3 %collective-permute-start.33 = (bf16[2,192,768]{2,1,0:T(8,128)(2,1)S(1)}, bf16[2,192,768]{2,1,0:T(8,128)(2,1)S(1)}, u32[]{:S(2)}, u32[]{:S(2)}) collective-permute-start(bf16[2,192,768]{2,1,0:T(8,128)(2,1)S(1)} %fusion.5.refs_6_), channel_id=1, source_target_pairs={{0,8},{4,12},{8,0},{12,4},{1,9},{5,13},{9,1},{13,5},{2,10},{6,14},... | collective-permute-start | bytes 1769480 | tf_op jit(solution)/shard_map/ppermute | solution.py:834
  182.2 28.5 %collective-permute-start.31 = (bf16[384,768]{1,0:T(8,128)(2,1)S(1)}, bf16[384,768]{1,0:T(8,128)(2,1)}, u32[]{:S(2)}, u32[]{:S(2)}) collective-permute-start(bf16[384,768]{1,0:T(8,128)(2,1)S(1)} %copy-done.11), channel_id=1, source_target_pairs={{0,16},{16,0},{1,17},{17,1},{2,18},{18,2},{3,19},{19,3},{4,20},{20... | collective-permute-start | bytes 1769480 | tf_op jit(solution)/shard_map/ppermute | solution.py:957
  195.8 28.2 %collective-permute-start.28 = (bf16[384,768]{1,0:T(8,128)(2,1)}, bf16[384,768]{1,0:T(8,128)(2,1)}, u32[]{:S(2)}, u32[]{:S(2)}) collective-permute-start(bf16[384,768]{1,0:T(8,128)(2,1)} %get-tuple-element.121), channel_id=1, source_target_pairs={{1,0},{2,1},{3,2},{5,4},{6,5},{7,6},{9,8},{10,9},{11,10},{13,12},{... | collective-permute-start | bytes 1769480 | tf_op jit(solution)/shard_map/ppermute | solution.py:975
  202.0 51.6 %all-to-all-start = ((bf16[4,192,768]{2,1,0:T(8,128)(2,1)}), bf16[4,192,768]{2,1,0:T(8,128)(2,1)S(1)}, u32[]{:S(2)}, u32[]{:S(2)}) async-start(bf16[4,192,768]{2,1,0:T(8,128)(2,1)} %pad_maximum_fusion.1.refs_11_), calls=%async_computation | async-start | bytes 2359296 | tf_op jit(solution)/shard_map/all_to_all | solution.py:973
  226.1 27.5 %collective-permute-start.29 = (bf16[384,768]{1,0:T(8,128)(2,1)}, bf16[384,768]{1,0:T(8,128)(2,1)S(1)}, u32[]{:S(2)}, u32[]{:S(2)}) collective-permute-start(bf16[384,768]{1,0:T(8,128)(2,1)} %add_convert_fusion), channel_id=1, source_target_pairs={{1,0},{2,1},{3,2},{5,4},{6,5},{7,6},{9,8},{10,9},{11,10},{13,12},{... | collective-permute-start | bytes 1769480 | tf_op jit(solution)/shard_map/ppermute | solution.py:979
  250.2 16.0 %collective-permute-start.42 = (bf16[192,384]{1,0:T(8,128)(2,1)}, bf16[192,384]{1,0:T(8,128)(2,1)}, u32[]{:S(2)}, u32[]{:S(2)}) collective-permute-start(bf16[192,384]{1,0:T(8,128)(2,1)} %get-tuple-element.165), channel_id=1, source_target_pairs={{0,2},{1,3},{2,0},{3,1},{4,6},{5,7},{6,4},{7,5},{8,10},{9,11},{10,... | collective-permute-start | bytes 442376 | tf_op jit(solution)/shard_map/ppermute | solution.py:856
  (69 other events, 695.8 us)
where the time goes:
time: 283 us; the launch traced here: 278 us
  Pallas kernels  106 us (37%)
  waiting for transfers between devices  63.5 us (22%)
  starting transfers between devices  62.9 us (22%)
  other arithmetic  23.7 us (8%)
  local copies, waits for them, and re-layouts  17.4 us (6%)
  between operations  4.08 us (1%)
    ppermute x4, waiting for transfers between devices, xor_sum(): lax.ppermute(values, axis, [(i, i ^ 1 << bit) for i in range(size)])  19.5 us
    pallas_call x1, Pallas kernels, attend_backward(): pl.pallas_call(with_deps(functools.partial(attend_backward_kernel, layout...  19.4 us
    pallas_call x1, Pallas kernels, front(): pl.pallas_call(with_deps(functools.partial(front_kernel, layout), 12, len...  16.4 us
    ppermute x6, waiting for transfers between devices, gather_cols(): lax.ppermute(block, 'col', shift(n_col, k))  16.2 us
    pallas_call x1, Pallas kernels, mlp(): pl.pallas_call(with_deps(functools.partial(mlp_kernel, layout), 5 + len(p...  15.6 us
    ppermute x6, starting transfers between devices, gather_cols(): lax.ppermute(block, 'col', shift(n_col, k))  13.2 us
    ppermute x2, starting transfers between devices, shards(): seen.insert(0, lax.ppermute(sent, 'col', step_right))  12.3 us
    ppermute x2, waiting for transfers between devices, shards(): seen.insert(0, lax.ppermute(sent, 'col', step_right))  11 us
  transfers between devices with their start and end apart: 49, of which 14 were waited for; matrix products, arithmetic and copies ran while one was open for 10% of the time, Pallas kernels for 33%

commit v1 on v0

--- a/solution.py
+++ b/solution.py
@@ -14,7 +14,7 @@
 Q_ROWS = 128
 NEG = -1e30
 SCALE = HEAD_DIM ** (-0.5)
-VMEM_LIMIT = 56 * 1024 * 1024
+VMEM_LIMIT = 28 * 1024 * 1024
 LOW = jnp.bfloat16
 COST = pl.CostEstimate(flops=1000, bytes_accessed=1000, transcendentals=0)
 F32 = jnp.float32
@@ -465,8 +465,11 @@
     h_t[:, rows:] = h2_ref[...].T
     slots = grad_slots(layout)
     for col in range(layout.n_col):
-        step = lax.rem(layout.col(info) + (layout.n_col - col), layout.n_col)
-        lanes = pl.ds(pl.multiple_of(step * half, half), half)
+        away = lax.rem(
+            layout.col(info) + layout.n_col - jnp.bitwise_xor(layout.col(info), jnp.int32(col)),
+            layout.n_col,
+        )
+        lanes = pl.ds(pl.multiple_of(away * half, half), half)
         for j, (left, right) in enumerate(((dy_t, hid_ref), (h_t, dgate_ref), (h_t, dup_ref))):
             for a in range(layout.n_row):
                 out, index = slots[a, col]
@@ -792,14 +795,39 @@
     ]
 
 
+def gather_halves(layout, plane):
+    if layout.n_row != 4:
+        return [plane]
+    cut = layout.n_col // 2
+    return [plane] + [
+        lax.ppermute(half, "row", [(i, i ^ by) for i in range(4)])
+        for by in (1, 2)
+        for half in (plane[:cut], plane[cut:])
+    ]
+
+
 def gather_corner(layout, sides):
     if layout.n_row != 4:
         return [lax.all_gather(sides[0], "row", axis=0, tiled=True)]
-    return sides + [lax.ppermute(sides[1], "row", [(i, i ^ 2) for i in range(4)])]
+    if len(sides) == 3:
+        return sides + [lax.ppermute(sides[1], "row", [(i, i ^ 2) for i in range(4)])]
+    return sides + [
+        lax.ppermute(sides[1], "row", [(i, i ^ 2) for i in range(4)]),
+        lax.ppermute(sides[4], "row", [(i, i ^ 1) for i in range(4)]),
+    ]
 
 
 def both_cores(pieces):
     return pieces + [lax.ppermute(piece, "ba", SWAP) for piece in pieces]
+
+
+def add_blocks(inputs, outputs, *deps):
+    inputs = after(inputs, *deps) if deps else inputs
+    return [
+        jnp.stack([add_up([inputs[which][index] for which, index in terms]) for terms in blocks])
+        .astype(LOW)
+        for blocks in outputs
+    ]
 
 
 def plus(left, right):
@@ -816,14 +844,17 @@
     )
 
 
-def scatter_next(layout, grads, got):
+def scatter_next(layout, grads, got, *deps):
     if layout.n_row != 4:
         return got
-    got_x, got_y = got
-    _, _, _, on_y, on_x = grads
-    return (
-        plus(on_y, got_x[1]).astype(LOW),
-        plus(on_x, got_y[1]).astype(LOW),
+    cut = layout.n_col // 2
+    return add_blocks(
+        [grads[3], got[0], grads[4], got[1]],
+        [
+            [[(0, k), (1, (1, k))] for k in range(cut)],
+            [[(2, k), (3, (1, k))] for k in range(layout.n_col - cut)],
+        ],
+        *deps,
     )
 
 
@@ -836,18 +867,19 @@
     )
 
 
-def scatter_plane(layout, grads, got, crossed):
+def scatter_plane(layout, grads, got, crossed, groups, *deps):
     if layout.n_row != 4:
-        return list(crossed[0])
-    from_y, from_x = crossed
+        return [jnp.stack([crossed[0][k] for k in group]) for group in groups]
     cut = layout.n_col // 2
-    own = grads[0]
-    return [
-        (plus(own[k], got[0][0, k]) + from_y[k].astype(F32)).astype(LOW)
-        if k < cut
-        else (plus(own[k], got[1][0, k - cut]) + from_x[k - cut].astype(F32)).astype(LOW)
-        for k in range(layout.n_col)
-    ]
+
+    def terms(k):
+        if k < cut:
+            return [(0, k), (1, (0, k)), (3, k)]
+        return [(0, k), (2, (0, k - cut)), (4, k - cut)]
+
+    return add_blocks(
+        [grads[0], *got, *crossed], [[terms(k) for k in group] for group in groups], *deps
+    )
 
 
 def scatter_cols(layout, plane):
@@ -913,24 +945,24 @@
 
     attn_cols = gather_cols(layout, attn_block)
     normed = norm(tokens, gain_attn[None])
+    mlp_cols = gather_cols(layout, after(mlp_block, normed, *attn_cols))
     dy_other = lax.ppermute(cotangent, "ba", SWAP)
     dy_t, = turn([[cotangent, dy_other]])
-    mlp_cols = gather_cols(layout, after(mlp_block, normed, *attn_cols))
     attn_rows = gather_corner(layout, gather_sides(layout, jnp.stack(attn_cols)))
     seen = [normed]
     for hop in range(hops):
-        sent = after(seen[0], dy_t, cosine, sine, *mlp_cols) if hop == 0 else seen[0]
+        sent = after(seen[0], *mlp_cols) if hop == 0 else seen[0]
         seen.insert(0, lax.ppermute(sent, "col", step_right))
-    mlp_plane = after(jnp.stack(mlp_cols), *attn_rows)
+    mlp_plane = after(jnp.stack(mlp_cols), cosine, sine, dy_t, *attn_rows)
     attn_pieces = both_cores(attn_rows)
     mlp_sides = gather_sides(layout, mlp_plane)
 
     w_q, w_k, w_v, w_o_t, q, k_near, v_near = prepare(
         layout, info, seen[1:], cosine[rows:], sine[rows:], attn_pieces
     )
+    mlp_pieces = gather_corner(layout, after(mlp_sides, q))
     seen_other = [lax.ppermute(block, "ba", SWAP) for block in seen]
     near_t, = turn([[*seen[1:], *seen_other[1:]]], q)
-    mlp_pieces = gather_corner(layout, after(mlp_sides, near_t))
     k, v, heads, middle, h2, lse = front(
         layout, info, seen[0], cosine[:rows], sine[:rows], tokens, gain_mlp[None], q, k_near,
         v_near, w_k, w_v, w_o_t, near_t,
@@ -952,7 +984,7 @@
     dq, keep_long, send_long = attend_backward(
         layout, info, 0, 1, q, k, v, d_heads, lse, inner, cosine, sine, heads_other, seen_other[0]
     )
-    sums_mlp = scatter_next(layout, grads_mlp, after(got_mlp, dq))
+    sums_mlp = scatter_next(layout, grads_mlp, got_mlp, dq)
     got_long = lax.ppermute(send_long, "ba", SWAP)
     dq_other = lax.ppermute(dq, "ba", SWAP)
     crossed_mlp = scatter_cross(layout, sums_mlp)
@@ -965,30 +997,37 @@
     )
     gains = jnp.concatenate([dgain_attn, dgain_mlp])
     gains = gains + lax.ppermute(gains, "ba", SWAP)
-    plane_mlp = jnp.stack(scatter_plane(layout, grads_mlp, got_mlp, after(crossed_mlp, far)))
+    passed, kept = scatter_plane(
+        layout, grads_mlp, got_mlp, crossed_mlp, [range(1, n_col, 2), range(0, n_col, 2)], far
+    )
+    bits = n_row.bit_length() - 1
     grads_attn = attend_grads(
         layout, info, near_t, far_t, short_t, keep_long, got_long, dq, dq_other, heads,
-        heads_other, gains, plane_mlp,
-    )
-    blocks_mlp = lax.all_to_all(plane_mlp, "col", 0, 0, tiled=True)
+        heads_other, gains, kept,
+    )
+    near_sum = lax.ppermute(passed, "col", [(i, i ^ 1) for i in range(n_col)])
     got_attn = scatter_start(layout, grads_attn)
     arrived = lax.ppermute(far, "col", step_left)
     travelling = near
     for hop in range(1, hops):
-        travelling = plus(near[(hop - 1) * rows : hop * rows], arrived).astype(LOW)
-        arrived = lax.ppermute(travelling, "col", step_left)
-    half_bits = (n_row.bit_length() - 1) // 2
-    gains = xor_sum(after(gains, grads_attn[0]), "row", n_row, range(half_bits))
-    sums_attn = scatter_next(layout, grads_attn, after(got_attn, travelling, gains))
+        travelling, = add_blocks(
+            [near[(hop - 1) * rows : hop * rows][None], arrived[None]], [[[(0, 0), (1, 0)]]]
+        )
+        arrived = lax.ppermute(travelling[0], "col", step_left)
+    gains = xor_sum(after(gains, grads_attn[0]), "row", n_row, range(bits // 2))
+    sums_attn = scatter_next(layout, grads_attn, got_attn, travelling, gains)
     crossed_attn = scatter_cross(layout, sums_attn)
-    gains = xor_sum(
-        after(gains, *sums_attn), "row", n_row, range(half_bits, n_row.bit_length() - 1)
-    )
-    plane_attn = scatter_plane(layout, grads_attn, got_attn, after(crossed_attn, gains))
+    held = plus(kept, near_sum)
+    part, away = held[0], held[1:]
+    far_sum = lax.ppermute(after(away.astype(LOW), *sums_attn), "col", [(i, i ^ 2) for i in range(n_col)])
+    gains = xor_sum(after(gains, *sums_attn), "row", n_row, range(bits // 2, bits))
+    plane_attn = scatter_plane(
+        layout, grads_attn, got_attn, crossed_attn, [[k] for k in range(n_col)], gains
+    )
+    plane_attn = [block[0] for block in plane_attn]
     blocks_attn = scatter_cols(layout, plane_attn)
     d_h1 = own + after(arrived, *plane_attn).astype(F32)
-    blocks_mlp = after(blocks_mlp, *plane_attn)
-    part = add_up([blocks_mlp[k] for k in range(n_col)])
+    part = part + after(far_sum, *plane_attn)[0].astype(F32)
     x = tokens.astype(F32)
     scale = lax.rsqrt(jnp.mean(x * x, axis=1, keepdims=True) + EPSILON)
     weighted = d_h1 * gain_attn[None, :]

time: 283 us -> 257 us (0.908)
  Pallas kernels: 106 us -> 79.2 us
  local copies, waits for them, and re-layouts: 17.4 us -> 25.6 us
  other arithmetic: 23.7 us -> 16.7 us
  waiting for transfers between devices: 63.5 us -> 57 us
  starting transfers between devices: 62.9 us -> 68.8 us
    unnamed x90 -> x106, local copies, waits for them, and re-layouts: 9.26 us -> 20.5 us
    ppermute x4, starting transfers between devices: 5.12 us -> 13.6 us  [xor_sum(): lax.ppermute(values, axis, [(i, i ^ 1 << bit) for i in range(size)])]
    all_to_all x1 -> x0, starting transfers between devices: 7.39 us -> none  [shards(): blocks_mlp = lax.all_to_all(plane_mlp, 'col', 0, 0, tiled=True)]
    convert_element_type x7 -> x1, other arithmetic: 7.24 us -> 0.15 us  [add_blocks(): return [jnp.stack([add_up([inputs[which][index] for which, index in terms...]
    ppermute x2, waiting for transfers between devices: 11 us -> 4.13 us  [shards(): seen.insert(0, lax.ppermute(sent, 'col', step_right))]
    ppermute x6, waiting for transfers between devices: 16.2 us -> 11.2 us  [gather_cols(): lax.ppermute(block, 'col', shift(n_col, k))]
    pallas_call x2, Pallas kernels: 6.29 us -> 2.49 us  [turn(): pl.pallas_call(with_deps(functools.partial(turn_kernel, counts), len(arra...]
    ppermute x3, waiting for transfers between devices: 8.18 us -> 4.4 us  [scatter_cols(): lax.ppermute(plane[k], 'col', shift(n_col, n_col - k))]
  transfers between devices with their start and end apart: 49 -> 50, of which waited for: 14 -> 16; matrix products, arithmetic and copies ran while one was open for 10% -> 7% of each run, Pallas kernels for 33% -> 26%
where the time goes in v1:
time: 257 us; the launch traced here: 252 us
  Pallas kernels  79.2 us (31%)
  starting transfers between devices  68.8 us (27%)
  waiting for transfers between devices  57 us (22%)
  local copies, waits for them, and re-layouts  25.6 us (10%)
  other arithmetic  16.7 us (6%)
  between operations  4.55 us (2%)
    unnamed x106, local copies, waits for them, and re-layouts  20.5 us
    ppermute x4, waiting for transfers between devices, xor_sum(): lax.ppermute(values, axis, [(i, i ^ 1 << bit) for i in range(size)])  19.2 us
    pallas_call x1, Pallas kernels, attend_backward(): pl.pallas_call(with_deps(functools.partial(attend_backward_kernel, layout...  15.8 us
    ppermute x2, starting transfers between devices, shards(): seen.insert(0, lax.ppermute(sent, 'col', step_right))  15.3 us
    pallas_call x1, Pallas kernels, front(): pl.pallas_call(with_deps(functools.partial(front_kernel, layout), 12, len...  14.1 us
    ppermute x4, starting transfers between devices, xor_sum(): lax.ppermute(values, axis, [(i, i ^ 1 << bit) for i in range(size)])  13.6 us
    ppermute x6, starting transfers between devices, gather_cols(): lax.ppermute(block, 'col', shift(n_col, k))  13.1 us
    pallas_call x1, Pallas kernels, mlp(): pl.pallas_call(with_deps(functools.partial(mlp_kernel, layout), 5 + len(p...  13 us
  transfers between devices with their start and end apart: 50, of which 16 were waited for; matrix products, arithmetic and copies ran while one was open for 7% of the time, Pallas kernels for 26%

profile of v1, /device:TPU:0, one launch (start us, length us, event | category | flops | bytes accessed | tf_op | source)
XLA Modules:
  0.0 251.9 jit_solution(15741378579834792706)
XLA Ops:
  2.9 3.1 %collective-permute-start = (bf16[192,384]{1,0:T(8,128)(2,1)S(1)}, bf16[192,384]{1,0:T(8,128)(2,1)S(1)}, u32[]{:S(2)}, u32[]{:S(2)}) collective-permute-start(bf16[192,384]{1,0:T(8,128)(2,1)S(1)} %maximum_select_fusion), channel_id=1, source_target_pairs={{0,1},{1,2},{2,3},{3,0},{4,5},{5,6},{6,7},{7,4},{8,9},{9,10},{10,1... | collective-permute-start | bytes 442376 | tf_op jit(solution)/shard_map/ppermute | solution.py:787
  13.9 4.4 %collective-permute-done.1 = bf16[192,384]{1,0:T(8,128)(2,1)S(1)} collective-permute-done((bf16[192,384]{1,0:T(8,128)(2,1)S(1)}, bf16[192,384]{1,0:T(8,128)(2,1)S(1)}, u32[]{:S(2)}, u32[]{:S(2)}) %collective-permute-start.1) | collective-permute-done | bytes 147488 | tf_op jit(solution)/shard_map/ppermute | solution.py:787
  20.7 3.7 %collective-permute-start.3 = (bf16[192,768]{1,0:T(8,128)(2,1)S(1)}, bf16[192,768]{1,0:T(8,128)(2,1)S(1)}, u32[]{:S(2)}, u32[]{:S(2)}) collective-permute-start(bf16[192,768]{1,0:T(8,128)(2,1)S(1)} %pad_maximum_fusion.8), channel_id=1, source_target_pairs={{0,1},{1,2},{2,3},{3,0},{4,5},{5,6},{6,7},{7,4},{8,9},{9,10},{10,1... | collective-permute-start | bytes 884744 | tf_op jit(solution)/shard_map/ppermute | solution.py:787
  38.3 5.8 %collective-permute-done.4 = bf16[192,768]{1,0:T(8,128)(2,1)S(1)} collective-permute-done((bf16[192,768]{1,0:T(8,128)(2,1)S(1)}, bf16[192,768]{1,0:T(8,128)(2,1)S(1)}, u32[]{:S(2)}, u32[]{:S(2)}) %collective-permute-start.4) | collective-permute-done | bytes 294944 | tf_op jit(solution)/shard_map/ppermute | solution.py:787
  44.0 9.5 %collective-permute-start.6 = (bf16[384,768]{1,0:T(8,128)(2,1)S(1)}, bf16[384,768]{1,0:T(8,128)(2,1)}, u32[]{:S(2)}, u32[]{:S(2)}) collective-permute-start(bf16[384,768]{1,0:T(8,128)(2,1)S(1)} %copy-done.2), channel_id=1, source_target_pairs={{0,1},{1,2},{2,3},{4,5},{5,6},{6,7},{8,9},{9,10},{10,11},{12,13},{... | collective-permute-start | bytes 1769480 | tf_op jit(solution)/shard_map/ppermute | solution.py:955
  55.1 3.0 %collective-permute-done.10.refs_8_ = bf16[4,192,384]{2,1,0:T(8,128)(2,1)} collective-permute-done((bf16[4,192,384]{2,1,0:T(8,128)(2,1)}, bf16[4,192,384]{2,1,0:T(8,128)(2,1)}, u32[]{:S(2)}, u32[]{:S(2)}) %collective-permute-start.10) | collective-permute-done | bytes 589856 | tf_op jit(solution)/shard_map/ppermute | solution.py:813
  61.5 4.1 %collective-permute-done.6.refs_1_.refs_0_.refs_2_ = bf16[384,768]{1,0:T(8,128)(2,1)} collective-permute-done((bf16[384,768]{1,0:T(8,128)(2,1)S(1)}, bf16[384,768]{1,0:T(8,128)(2,1)}, u32[]{:S(2)}, u32[]{:S(2)}) %collective-permute-start.6) | collective-permute-done | bytes 589856 | tf_op jit(solution)/shard_map/ppermute | solution.py:955
  67.9 5.8 %collective-permute-start.7 = (bf16[384,768]{1,0:T(8,128)(2,1)}, bf16[384,768]{1,0:T(8,128)(2,1)}, u32[]{:S(2)}, u32[]{:S(2)}) collective-permute-start(bf16[384,768]{1,0:T(8,128)(2,1)} %collective-permute-done.6.refs_1_.refs_0_.refs_2_), channel_id=1, source_target_pairs={{0,1},{1,2},{2,3},{4,5},{5,6},{6,7},{8,9},{9,10},{10,11},{12,13},{... | collective-permute-start | bytes 1769480 | tf_op jit(solution)/shard_map/ppermute | solution.py:955
  75.8 8.7 %prepare.1 = (bf16[768,768]{1,0:T(8,128)(2,1)S(1)}, bf16[768,768]{1,0:T(8,128)(2,1)S(1)}, bf16[768,768]{1,0:T(8,128)(2,1)S(1)}, bf16[768,768]{1,0:T(8,128)(2,1)S...) custom-call(s32[8]{0:T(128)S(1)} %concatenate.54.refs_0_, ...), custom_call_target="tpu_custom_call" | custom-call | flops 1000 | bytes 1000 | tf_op jit(solution)/shard_map/prepare/pallas_call | solution.py:191
  89.6 14.1 %front.1 = (bf16[1152,768]{1,0:T(8,128)(2,1)S(1)}, bf16[1152,768]{1,0:T(8,128)(2,1)S(1)}, bf16[384,768]{1,0:T(8,128)(2,1)}, f32[384,768]{1,0:T(8,128)S(1)}, bf16...) custom-call(s32[8]{0:T(128)S(1)} %concatenate.54.refs_0_, bf16[384,768]{1,0:T(8,128)(2,1)} %collective-permute-done.7.refs_1_, ...), custom_call_target="tpu_custom_call" | custom-call | flops 1000 | bytes 1000 | tf_op jit(solution)/shard_map/front/pallas_call | solution.py:276
  109.1 4.6 %collective-permute-done.21.refs_8_ = bf16[4,192,768]{2,1,0:T(8,128)(2,1)S(1)} collective-permute-done((bf16[4,192,768]{2,1,0:T(8,128)(2,1)}, bf16[4,192,768]{2,1,0:T(8,128)(2,1)S(1)}, u32[]{:S(2)}, u32[]{:S(2)}) %collective-permute-start.21) | collective-permute-done | bytes 1179680 | tf_op jit(solution)/shard_map/ppermute | solution.py:813
  113.7 13.0 %mlp.1 = (f32[384,768]{1,0:T(8,128)S(1)}, f32[384,768]{1,0:T(8,128)S(1)}, bf16[2,384,768]{2,1,0:T(8,128)(2,1)}, bf16[768,1024]{1,0:T(8,128)(2,1)S(1)}, bf16[768,...) custom-call(s32[8]{0:T(128)S(1)} %concatenate.54.refs_0_, bf16[384,768]{1,0:T(8,128)(2,1)S(1)} %get-tuple-element.99.refs_1_.refs_4_, ...), custom_call_target="tpu_custom_call" | custom-call | flops 1000 | bytes 1000 | tf_op jit(solution)/shard_map/mlp/pallas_call | solution.py:360
  127.8 5.8 %mlp_grads.1 = (bf16[4,192,768]{2,1,0:T(8,128)(2,1)S(1)}, bf16[2,2,192,768]{3,2,1,0:T(8,128)(2,1)}, bf16[2,2,192,768]{3,2,1,0:T(8,128)(2,1)}, bf16[2,192,768]{2,1,0:T(8,128)(2,1)S(1)}, bf16[2,192,768]{2,1,0:T(8,128)(2,1)S(1)}) custom-call(s32[8]{0:T(128)S(1)} %concatenate.54.refs_0_, bf16[768,1024]{1,0:T(8,128)(2,1)S(1)} %get-tuple-element.107.refs_1_, ...), custom_call_target="tpu_custom_call" | custom-call | flops 1000 | bytes 1000 | tf_op jit(solution)/shard_map/mlp_grads/pallas_call | solution.py:486
  147.1 4.3 %middle_grads.1 = (bf16[384,768]{1,0:T(8,128)(2,1)}, f32[384,768]{1,0:T(8,128)S(1)}, bf16[384,768]{1,0:T(8,128)(2,1)S(1)}, bf16[384,768]{1,0:T(8,128)(2,1)S(1)},...) custom-call(f32[384,768]{1,0:T(8,128)S(1)} %copy-done.31, bf16[384,768]{1,0:T(8,128)(2,1)S(1)} %copy-done.7, ...), custom_call_target="tpu_custom_call" | custom-call | flops 1000 | bytes 1000 | tf_op jit(solution)/shard_map/middle_grads/pallas_call | solution.py:413
  151.5 15.8 %attend_backward.1 = (bf16[384,768]{1,0:T(8,128)(2,1)S(1)}, bf16[1152,768]{1,0:T(8,128)(2,1)S(1)}, bf16[1152,768]{1,0:T(8,128)(2,1)S(1)}) custom-call(s32[9]{0:T(128)S(1)} %concatenate.64.refs_0_, bf16[384,768]{1,0:T(8,128)(2,1)S(1)} %copy-done.9, bf16[1152,768]{1,0:T(8,128)(2,1)S(1)} %copy-done.24, bf16[1152,768]{1,0:T(8,128)(2,1)S(1)} %copy-done.26, ...), custom_call_target="tpu_custom_call" | custom-call | flops 1000 | bytes 1000 | tf_op jit(solution)/shard_map/attend_backward/pallas_call | solution.py:638
  175.0 4.9 %seen_grads.1 = (bf16[384,768]{1,0:T(8,128)(2,1)S(1)}, bf16[384,768]{1,0:T(8,128)(2,1)S(1)}, f32[384,768]{1,0:T(8,128)S(1)}, f32[1,768]{1,0:T(1,128)S(1)}) custom-call(s32[8]{0:T(128)S(1)} %concatenate.54.refs_0_, bf16[384,768]{1,0:T(8,128)(2,1)} %collective-permute-done.7.refs_1_, bf16[384,768]{1,0:T(8,128)(2,1)} %collective-permute-done.6.refs_1_.refs_0_.refs_2_, ...), custom_call_target="tpu_custom_call" | custom-call | flops 1000 | bytes 1000 | tf_op jit(solution)/shard_map/seen_grads/pallas_call | solution.py:695
  181.3 3.4 %collective-permute-done.34 = bf16[2,192,768]{2,1,0:T(8,128)(2,1)S(1)} collective-permute-done((bf16[2,192,768]{2,1,0:T(8,128)(2,1)S(1)}, bf16[2,192,768]{2,1,0:T(8,128)(2,1)S(1)}, u32[]{:S(2)}, u32[]{:S(2)}) %collective-permute-start.34) | collective-permute-done | bytes 589856 | tf_op jit(solution)/shard_map/ppermute | solution.py:866
  184.7 2.6 %collective-permute-done.33 = bf16[2,192,768]{2,1,0:T(8,128)(2,1)S(1)} collective-permute-done((bf16[2,192,768]{2,1,0:T(8,128)(2,1)S(1)}, bf16[2,192,768]{2,1,0:T(8,128)(2,1)S(1)}, u32[]{:S(2)}, u32[]{:S(2)}) %collective-permute-start.33) | collective-permute-done | bytes 589856 | tf_op jit(solution)/shard_map/ppermute | solution.py:865
  189.2 5.6 %attend_grads.1 = (bf16[4,192,384]{2,1,0:T(8,128)(2,1)S(1)}, bf16[2,2,192,384]{3,2,1,0:T(8,128)(2,1)S(1)}, bf16[2,2,192,384]{3,2,1,0:T(8,128)(2,1)S(1)}, bf16[2,...) custom-call(s32[8]{0:T(128)S(1)} %concatenate.54.refs_0_, bf16[768,1536]{1,0:T(8,128)(2,1)S(1)} %turn.2.refs_12_.refs_5_.refs_1_, ...), custom_call_target="tpu_custom_call" | custom-call | flops 1000 | bytes 1000 | tf_op jit(solution)/shard_map/attend_grads/pallas_call | solution.py:760
  199.1 11.6 %collective-permute-done.37 = f32[2,768]{1,0:T(2,128)S(1)} collective-permute-done((f32[2,768]{1,0:T(2,128)S(1)}, f32[2,768]{1,0:T(2,128)S(1)}, u32[]{:S(2)}, u32[]{:S(2)}) %collective-permute-start.37) | collective-permute-done | bytes 6176 | tf_op jit(solution)/shard_map/ppermute | solution.py:901
  217.0 3.9 %collective-permute-done.40 = f32[2,768]{1,0:T(2,128)S(1)} collective-permute-done((f32[2,768]{1,0:T(2,128)S(1)}, f32[2,768]{1,0:T(2,128)S(1)}, u32[]{:S(2)}, u32[]{:S(2)}) %collective-permute-start.40) | collective-permute-done | bytes 6176 | tf_op jit(solution)/shard_map/ppermute | solution.py:901
  225.2 9.8 %collective-permute-start.46 = (f32[2,768]{1,0:T(2,128)S(1)}, f32[2,768]{1,0:T(2,128)S(1)}, u32[]{:S(2)}, u32[]{:S(2)}) collective-permute-start(f32[2,768]{1,0:T(2,128)S(1)} %add.214), channel_id=1, source_target_pairs={{0,1},{1,0},{2,3},{3,2},{4,5},{5,4},{6,7},{7,6},{8,9},{9,8},{10,11... | collective-permute-start | bytes 18440 | tf_op jit(solution)/shard_map/ppermute | solution.py:901
  236.8 4.4 %collective-permute-done.43 = bf16[192,384]{1,0:T(8,128)(2,1)S(1)} collective-permute-done((bf16[192,384]{1,0:T(8,128)(2,1)S(1)}, bf16[192,384]{1,0:T(8,128)(2,1)S(1)}, u32[]{:S(2)}, u32[]{:S(2)}) %collective-permute-start.43) | collective-permute-done | bytes 147488 | tf_op jit(solution)/shard_map/ppermute | solution.py:888
  242.2 3.7 %collective-permute-done.49 = f32[2,768]{1,0:T(2,128)S(1)} collective-permute-done((f32[2,768]{1,0:T(2,128)S(1)}, f32[2,768]{1,0:T(2,128)S(1)}, u32[]{:S(2)}, u32[]{:S(2)}) %collective-permute-start.49) | collective-permute-done | bytes 6176 | tf_op jit(solution)/shard_map/ppermute | solution.py:901
  (247 shorter events, 91.8 us)
Async XLA Ops:
  9.9 44.8 %collective-permute-start.18 = (bf16[384,768]{1,0:T(8,128)(2,1)}, bf16[384,768]{1,0:T(8,128)(2,1)S(1)}, u32[]{:S(2)}, u32[]{:S(2)}) collective-permute-start(bf16[384,768]{1,0:T(8,128)(2,1)} %refs_1_.1), channel_id=1, source_target_pairs={{0,16},{16,0},{1,17},{17,1},{2,18},{18,2},{3,19},{19,3},{4,20},{20... | collective-permute-start | bytes 1769480 | tf_op jit(solution)/shard_map/ppermute | solution.py:949
  19.2 15.5 %collective-permute-start.8 = (bf16[4,192,384]{2,1,0:T(8,128)(2,1)}, bf16[4,192,384]{2,1,0:T(8,128)(2,1)}, u32[]{:S(2)}, u32[]{:S(2)}) collective-permute-start(bf16[4,192,384]{2,1,0:T(8,128)(2,1)} %pad_maximum_fusion.1.refs_5_), channel_id=1, source_target_pairs={{0,4},{4,0},{8,12},{12,8},{1,5},{5,1},{9,13},{13,9},{2,6},{6,2},{1... | collective-permute-start | bytes 1769480 | tf_op jit(solution)/shard_map/ppermute | solution.py:794
  28.3 15.8 %collective-permute-start.4 = (bf16[192,768]{1,0:T(8,128)(2,1)S(1)}, bf16[192,768]{1,0:T(8,128)(2,1)S(1)}, u32[]{:S(2)}, u32[]{:S(2)}) collective-permute-start(bf16[192,768]{1,0:T(8,128)(2,1)S(1)} %pad_maximum_fusion.8), channel_id=1, source_target_pairs={{0,2},{1,3},{2,0},{3,1},{4,6},{5,7},{6,4},{7,5},{8,10},{9,11},{10,... | collective-permute-start | bytes 884744 | tf_op jit(solution)/shard_map/ppermute | solution.py:787
  31.8 23.3 %collective-permute-start.9 = (bf16[4,192,384]{2,1,0:T(8,128)(2,1)}, bf16[4,192,384]{2,1,0:T(8,128)(2,1)}, u32[]{:S(2)}, u32[]{:S(2)}) collective-permute-start(bf16[4,192,384]{2,1,0:T(8,128)(2,1)} %pad_maximum_fusion.1.refs_5_), channel_id=1, source_target_pairs={{0,8},{4,12},{8,0},{12,4},{1,9},{5,13},{9,1},{13,5},{2,10},{6,14},... | collective-permute-start | bytes 1769480 | tf_op jit(solution)/shard_map/ppermute | solution.py:794
  34.6 23.4 %collective-permute-start.10 = (bf16[4,192,384]{2,1,0:T(8,128)(2,1)}, bf16[4,192,384]{2,1,0:T(8,128)(2,1)}, u32[]{:S(2)}, u32[]{:S(2)}) collective-permute-start(bf16[4,192,384]{2,1,0:T(8,128)(2,1)} %collective-permute-done.8.refs_6_), channel_id=1, source_target_pairs={{0,8},{4,12},{8,0},{12,4},{1,9},{5,13},{9,1},{13,5},{2,10},{6,14},... | collective-permute-start | bytes 1769480 | tf_op jit(solution)/shard_map/ppermute | solution.py:813
  44.0 16.1 %collective-permute-start.11 = (bf16[4,192,384]{2,1,0:T(8,128)(2,1)}, bf16[4,192,384]{2,1,0:T(8,128)(2,1)S(1)}, u32[]{:S(2)}, u32[]{:S(2)}) collective-permute-start(bf16[4,192,384]{2,1,0:T(8,128)(2,1)} %pad_maximum_fusion.1.refs_5_), channel_id=1, source_target_pairs={{0,16},{16,0},{1,17},{17,1},{2,18},{18,2},{3,19},{19,3},{4,20},{20... | collective-permute-start | bytes 1769480 | tf_op jit(solution)/shard_map/ppermute | solution.py:821
  44.0 21.5 %collective-permute-start.6 = (bf16[384,768]{1,0:T(8,128)(2,1)S(1)}, bf16[384,768]{1,0:T(8,128)(2,1)}, u32[]{:S(2)}, u32[]{:S(2)}) collective-permute-start(bf16[384,768]{1,0:T(8,128)(2,1)S(1)} %copy-done.2), channel_id=1, source_target_pairs={{0,1},{1,2},{2,3},{4,5},{5,6},{6,7},{8,9},{9,10},{10,11},{12,13},{... | collective-permute-start | bytes 1769480 | tf_op jit(solution)/shard_map/ppermute | solution.py:955
  58.1 27.6 %collective-permute-start.19 = (bf16[4,192,768]{2,1,0:T(8,128)(2,1)}, bf16[4,192,768]{2,1,0:T(8,128)(2,1)}, u32[]{:S(2)}, u32[]{:S(2)}) collective-permute-start(bf16[4,192,768]{2,1,0:T(8,128)(2,1)} %pad_maximum_fusion.refs_5_), channel_id=1, source_target_pairs={{0,4},{4,0},{8,12},{12,8},{1,5},{5,1},{9,13},{13,9},{2,6},{6,2},{1... | collective-permute-start | bytes 3538952 | tf_op jit(solution)/shard_map/ppermute | solution.py:794
  58.6 27.1 %collective-permute-start.20 = (bf16[4,192,768]{2,1,0:T(8,128)(2,1)}, bf16[4,192,768]{2,1,0:T(8,128)(2,1)}, u32[]{:S(2)}, u32[]{:S(2)}) collective-permute-start(bf16[4,192,768]{2,1,0:T(8,128)(2,1)} %pad_maximum_fusion.refs_5_), channel_id=1, source_target_pairs={{0,8},{4,12},{8,0},{12,4},{1,9},{5,13},{9,1},{13,5},{2,10},{6,14},... | collective-permute-start | bytes 3538952 | tf_op jit(solution)/shard_map/ppermute | solution.py:794
  66.4 20.9 %collective-permute-start.16 = (bf16[384,768]{1,0:T(8,128)(2,1)S(1)}, bf16[384,768]{1,0:T(8,128)(2,1)}, u32[]{:S(2)}, u32[]{:S(2)}) collective-permute-start(bf16[384,768]{1,0:T(8,128)(2,1)S(1)} %copy-done.2), channel_id=1, source_target_pairs={{0,16},{16,0},{1,17},{17,1},{2,18},{18,2},{3,19},{19,3},{4,20},{20... | collective-permute-start | bytes 1769480 | tf_op jit(solution)/shard_map/ppermute | solution.py:964
  66.9 20.4 %collective-permute-start.15 = (bf16[384,768]{1,0:T(8,128)(2,1)}, bf16[384,768]{1,0:T(8,128)(2,1)}, u32[]{:S(2)}, u32[]{:S(2)}) collective-permute-start(bf16[384,768]{1,0:T(8,128)(2,1)} %collective-permute-done.6.refs_1_.refs_0_.refs_2_), channel_id=1, source_target_pairs={{0,16},{16,0},{1,17},{17,1},{2,18},{18,2},{3,19},{19,3},{4,20},{20... | collective-permute-start | bytes 1769480 | tf_op jit(solution)/shard_map/ppermute | solution.py:964
  67.9 21.6 %collective-permute-start.7 = (bf16[384,768]{1,0:T(8,128)(2,1)}, bf16[384,768]{1,0:T(8,128)(2,1)}, u32[]{:S(2)}, u32[]{:S(2)}) collective-permute-start(bf16[384,768]{1,0:T(8,128)(2,1)} %collective-permute-done.6.refs_1_.refs_0_.refs_2_), channel_id=1, source_target_pairs={{0,1},{1,2},{2,3},{4,5},{5,6},{6,7},{8,9},{9,10},{10,11},{12,13},{... | collective-permute-start | bytes 1769480 | tf_op jit(solution)/shard_map/ppermute | solution.py:955
  85.7 28.0 %collective-permute-start.21 = (bf16[4,192,768]{2,1,0:T(8,128)(2,1)}, bf16[4,192,768]{2,1,0:T(8,128)(2,1)S(1)}, u32[]{:S(2)}, u32[]{:S(2)}) collective-permute-start(bf16[4,192,768]{2,1,0:T(8,128)(2,1)} %collective-permute-done.19.refs_6_), channel_id=1, source_target_pairs={{0,8},{4,12},{8,0},{12,4},{1,9},{5,13},{9,1},{13,5},{2,10},{6,14},... | collective-permute-start | bytes 3538952 | tf_op jit(solution)/shard_map/ppermute | solution.py:813
  136.4 31.0 %collective-permute-start.26 = (bf16[2,2,192,768]{3,2,1,0:T(8,128)(2,1)}, bf16[2,2,192,768]{3,2,1,0:T(8,128)(2,1)}, u32[]{:S(2)}, u32[]{:S(2)}) collective-permute-start(bf16[2,2,192,768]{3,2,1,0:T(8,128)(2,1)} %get-tuple-element.124), channel_id=1, source_target_pairs={{0,4},{4,0},{8,12},{12,8},{1,5},{5,1},{9,13},{13,9},{2,6},{6,2},{1... | collective-permute-start | bytes 3538952 | tf_op jit(solution)/shard_map/ppermute | solution.py:842
  136.9 30.5 %collective-permute-start.27 = (bf16[2,2,192,768]{3,2,1,0:T(8,128)(2,1)}, bf16[2,2,192,768]{3,2,1,0:T(8,128)(2,1)}, u32[]{:S(2)}, u32[]{:S(2)}) collective-permute-start(bf16[2,2,192,768]{3,2,1,0:T(8,128)(2,1)} %get-tuple-element.126), channel_id=1, source_target_pairs={{0,8},{4,12},{8,0},{12,4},{1,9},{5,13},{9,1},{13,5},{2,10},{6,14},... | collective-permute-start | bytes 3538952 | tf_op jit(solution)/shard_map/ppermute | solution.py:843
  167.5 21.7 %collective-permute-start.30 = (bf16[1152,768]{1,0:T(8,128)(2,1)S(1)}, bf16[1152,768]{1,0:T(8,128)(2,1)S(1)}, u32[]{:S(2)}, u32[]{:S(2)}) collective-permute-start(bf16[1152,768]{1,0:T(8,128)(2,1)S(1)} %get-tuple-element.121.refs_10_), channel_id=1, source_target_pairs={{0,16},{16,0},{1,17},{17,1},{2,18},{18,2},{3,19},{19,3},{4,20},{20... | collective-permute-start | bytes 5308424 | tf_op jit(solution)/shard_map/ppermute | solution.py:988
  172.7 16.5 %collective-permute-start.31 = (bf16[384,768]{1,0:T(8,128)(2,1)S(1)}, bf16[384,768]{1,0:T(8,128)(2,1)S(1)}, u32[]{:S(2)}, u32[]{:S(2)}) collective-permute-start(bf16[384,768]{1,0:T(8,128)(2,1)S(1)} %get-tuple-element.119.refs_8_.refs_6_), channel_id=1, source_target_pairs={{0,16},{16,0},{1,17},{17,1},{2,18},{18,2},{3,19},{19,3},{4,20},{20... | collective-permute-start | bytes 1769480 | tf_op jit(solution)/shard_map/ppermute | solution.py:989
  180.0 17.7 %collective-permute-start.28 = (bf16[384,768]{1,0:T(8,128)(2,1)S(1)}, bf16[384,768]{1,0:T(8,128)(2,1)S(1)}, u32[]{:S(2)}, u32[]{:S(2)}) collective-permute-start(bf16[384,768]{1,0:T(8,128)(2,1)S(1)} %get-tuple-element.134), channel_id=1, source_target_pairs={{1,0},{2,1},{3,2},{5,4},{6,5},{7,6},{9,8},{10,9},{11,10},{13,12},{... | collective-permute-start | bytes 1769480 | tf_op jit(solution)/shard_map/ppermute | solution.py:1010
  194.8 15.9 %collective-permute-start.35 = (bf16[2,2,192,384]{3,2,1,0:T(8,128)(2,1)S(1)}, bf16[2,2,192,384]{3,2,1,0:T(8,128)(2,1)S(1)}, u32[]{:S(2)}, u32[]{:S(2)}) collective-permute-start(bf16[2,2,192,384]{3,2,1,0:T(8,128)(2,1)S(1)} %get-tuple-element.144), channel_id=1, source_target_pairs={{0,4},{4,0},{8,12},{12,8},{1,5},{5,1},{9,13},{13,9},{2,6},{6,2},{1... | collective-permute-start | bytes 1769480 | tf_op jit(solution)/shard_map/ppermute | solution.py:842
  195.4 15.4 %collective-permute-start.36 = (bf16[2,2,192,384]{3,2,1,0:T(8,128)(2,1)S(1)}, bf16[2,2,192,384]{3,2,1,0:T(8,128)(2,1)S(1)}, u32[]{:S(2)}, u32[]{:S(2)}) collective-permute-start(bf16[2,2,192,384]{3,2,1,0:T(8,128)(2,1)S(1)} %get-tuple-element.145), channel_id=1, source_target_pairs={{0,8},{4,12},{8,0},{12,4},{1,9},{5,13},{9,1},{13,5},{2,10},{6,14},... | collective-permute-start | bytes 1769480 | tf_op jit(solution)/shard_map/ppermute | solution.py:843
  196.0 17.3 %collective-permute-start.44 = (bf16[2,192,768]{2,1,0:T(8,128)(2,1)S(1)}, bf16[2,192,768]{2,1,0:T(8,128)(2,1)S(1)}, u32[]{:S(2)}, u32[]{:S(2)}) collective-permute-start(bf16[2,192,768]{2,1,0:T(8,128)(2,1)S(1)} %pad_maximum_fusion.5), channel_id=1, source_target_pairs={{0,1},{1,0},{2,3},{3,2},{4,5},{5,4},{6,7},{7,6},{8,9},{9,8},{10,11... | collective-permute-start | bytes 1769480 | tf_op jit(solution)/shard_map/ppermute | solution.py:1008
  197.8 37.2 %collective-permute-start.29 = (bf16[384,768]{1,0:T(8,128)(2,1)S(1)}, bf16[384,768]{1,0:T(8,128)(2,1)S(1)}, u32[]{:S(2)}, u32[]{:S(2)}) collective-permute-start(bf16[384,768]{1,0:T(8,128)(2,1)S(1)} %add_convert_fusion), channel_id=1, source_target_pairs={{1,0},{2,1},{3,2},{5,4},{6,5},{7,6},{9,8},{10,9},{11,10},{13,12},{... | collective-permute-start | bytes 1769480 | tf_op jit(solution)/shard_map/ppermute | solution.py:1016
  221.1 15.6 %collective-permute-start.41 = (bf16[192,384]{1,0:T(8,128)(2,1)S(1)}, bf16[192,384]{1,0:T(8,128)(2,1)S(1)}, u32[]{:S(2)}, u32[]{:S(2)}) collective-permute-start(bf16[192,384]{1,0:T(8,128)(2,1)S(1)} %get-tuple-element.209), channel_id=1, source_target_pairs={{0,3},{1,0},{2,1},{3,2},{4,7},{5,4},{6,5},{7,6},{8,11},{9,8},{10,9... | collective-permute-start | bytes 442376 | tf_op jit(solution)/shard_map/ppermute | solution.py:888
  223.2 17.9 %collective-permute-start.43 = (bf16[192,384]{1,0:T(8,128)(2,1)S(1)}, bf16[192,384]{1,0:T(8,128)(2,1)S(1)}, u32[]{:S(2)}, u32[]{:S(2)}) collective-permute-start(bf16[192,384]{1,0:T(8,128)(2,1)S(1)} %get-tuple-element.190), channel_id=1, source_target_pairs={{0,1},{1,2},{2,3},{3,0},{4,5},{5,6},{6,7},{7,4},{8,9},{9,10},{10,1... | collective-permute-start | bytes 442376 | tf_op jit(solution)/shard_map/ppermute | solution.py:888
  (78 other events, 590.5 us)
